TPU v7x, 128 devices: a whole 4x4x4 slice. The times are simulated.
128 devices in a mesh: lat: 8 (over x, z_lo), lon: 16 (over z_hi, y, core).
Axes of the slice: x: 4, y: 4, z: 4 (z_hi: 2, z_lo: 2; z = z_hi * 2 + z_lo), core: 2. Of those that a mesh axis runs over, the one named last changes fastest.
Arguments:
- initial_state: bfloat16 [192, 384, 512], P('lat', 'lon'), may hold values from -6 to 6
- norm_gain: float32 [512], replicated, may hold values from 0.1 to 1.9
- input_weight: bfloat16 [512, 1536], replicated, may hold values from -2 to 2
- output_weight: bfloat16 [512, 512], replicated, may hold values from -0.25 to 0.25
- obs_in_weight: bfloat16 [512, 1024], replicated, may hold values from -0.25 to 0.25
- obs_out_weight: bfloat16 [1024, 256], replicated, may hold values from -0.1875 to 0.1875
- observed: bfloat16 [65536, 256], P(('lat', 'lon')), may hold values from -6 to 6
- error_scale: float32 [256], replicated, may hold values from 0.5 to 2
- foot_tile: int32 [65536, 1], P(('lat', 'lon')), may hold values from 0 to 127; in each aligned block of 512 rows (0 to 511, 512 to 1023, ...) at most 8 rows name the same one
- foot_cell: int32 [65536], P(('lat', 'lon')), may hold values from 0 to 575
- foot_count: int32 [128], P(('lat', 'lon')), may hold values from 1 to 512, 49152 in all
Outputs:
- gradient: float32 [192, 384, 512], P('lat', 'lon')
- misfit: float32 [65536], P(('lat', 'lon'))
Inputs may be any that keep to these rules, and one draw needn't show every extreme that they name: `foot_tile`: among the 512 footprints of one device at most 8 name the same tile. `foot_count`: the live footprints are the first slots of a device; the counts sum to 49152, and some device has all 512 live.
All inputs are finite; a program needn't handle non-finite values.
Results may differ from a plain program's by a relative error of at most 0.02.
The roundings to bfloat16 on the way count: a program that leaves them out, or rounds other values in their place, can miss the bound.
Values may be sent and summed in bfloat16 or wider, within the bound.
A program may use at most 128 MiB of HBM per device.

v0:
```python
import math

import jax
import jax.numpy as jnp
from jax import lax
from jax.sharding import PartitionSpec as P

HEADS = 8
WIN = 12


norm_eps = 1e-06


def extended_2(shard, sides, width):
    for axis, dim in sides:
        size, length = (lax.axis_size(axis), shard.shape[dim])
        up = [(i, (i + 1) % size) for i in range(size)]
        down = [(j, i) for i, j in up]
        last = lax.slice_in_dim(shard, length - width, length, axis=dim)
        first = lax.slice_in_dim(shard, 0, width, axis=dim)
        before = lax.ppermute(last, axis, up)
        after = lax.ppermute(first, axis, down)
        shard = jnp.concatenate([before, shard, after], axis=dim)
    return shard


def to_window_order(field):
    ext_rows, ext_cols, chans = field.shape
    bands = ext_rows // WIN
    nwin = ext_cols // WIN
    shaped = field.reshape(bands, WIN, nwin, WIN, chans).transpose(0, 2, 1, 3, 4)
    return shaped.reshape(bands, nwin, WIN * WIN, chans)


def from_window_order(blocks):
    bands, nwin, length, chans = blocks.shape
    shaped = blocks.reshape(bands, nwin, WIN, WIN, chans).transpose(0, 2, 1, 3, 4)
    return shaped.reshape(bands * WIN, nwin * WIN, chans)


def head_view(block, start, width):
    nwin, length, chans = block.shape
    return block[:, :, start : start + width].reshape(nwin, length, HEADS, width // HEADS)


def softmax_weights(queries, keys, row_valid):
    depth = queries.shape[-1]
    scores = jnp.einsum(
        "nqhe,nkhe->nhqk", queries, keys, preferred_element_type=jnp.float32
    ) / math.sqrt(depth)
    key_valid = jnp.repeat(row_valid, WIN)
    scores = jnp.where(key_valid[None, None, None, :], scores, jnp.float32(-1e30))
    top = jnp.max(scores, axis=-1, keepdims=True)
    expo = jnp.exp(scores - top)
    return expo / jnp.sum(expo, axis=-1, keepdims=True)


def band_forward(pieces):
    window_block, row_valid = pieces
    width = window_block.shape[-1] // 3
    queries = head_view(window_block, 0, width)
    keys = head_view(window_block, width, width)
    values = head_view(window_block, 2 * width, width)
    probs = softmax_weights(queries, keys, row_valid).astype(jnp.bfloat16)
    attended = jnp.einsum("nhqk,nkhe->nqhe", probs, values, preferred_element_type=jnp.float32)
    nwin, length = (attended.shape[0], attended.shape[1])
    return attended.astype(jnp.bfloat16).reshape(nwin, length, width)


def band_backward(pieces):
    window_block, grad_block, row_valid = pieces
    width = window_block.shape[-1] // 3
    queries = head_view(window_block, 0, width)
    keys = head_view(window_block, width, width)
    values = head_view(window_block, 2 * width, width)
    upstream = head_view(grad_block, 0, width)
    depth = queries.shape[-1]
    probs = softmax_weights(queries, keys, row_valid)
    value_grad = jnp.einsum(
        "nhqk,nqhe->nkhe", probs.astype(jnp.bfloat16), upstream, preferred_element_type=jnp.float32
    )
    prob_grad = jnp.einsum("nqhe,nkhe->nhqk", upstream, values, preferred_element_type=jnp.float32)
    inner = jnp.sum(probs * prob_grad, axis=-1, keepdims=True)
    score_grad = (probs * (prob_grad - inner) / math.sqrt(depth)).astype(jnp.bfloat16)
    query_grad = jnp.einsum("nhqk,nkhe->nqhe", score_grad, keys, preferred_element_type=jnp.float32)
    key_grad = jnp.einsum(
        "nhqk,nqhe->nkhe", score_grad, queries, preferred_element_type=jnp.float32
    )
    nwin, length = (query_grad.shape[0], query_grad.shape[1])
    return jnp.concatenate(
        [
            query_grad.astype(jnp.bfloat16).reshape(nwin, length, width),
            key_grad.astype(jnp.bfloat16).reshape(nwin, length, width),
            value_grad.astype(jnp.bfloat16).reshape(nwin, length, width),
        ],
        axis=-1,
    )


def shards(
    initial_state,
    norm_gain,
    input_weight,
    output_weight,
    obs_in_weight,
    obs_out_weight,
    observed,
    error_scale,
    foot_tile,
    foot_cell,
    foot_count,
):
    tile_rows, tile_cols, channels = initial_state.shape
    lat_count = lax.axis_size("lat")
    devices = lat_count * lax.axis_size("lon")
    foot_slots = observed.shape[0]
    capacity = 2 * foot_slots // devices
    buffer_rows = devices * capacity
    half_win = WIN // 2
    ext_rows = tile_rows + 2 * half_win
    band_count = ext_rows // WIN
    row_index = lax.axis_index("lat") * tile_rows - half_win + jnp.arange(ext_rows, dtype=jnp.int32)
    row_valid = (row_index >= 0) & (row_index < tile_rows * lat_count)
    valid_bands = row_valid.reshape(band_count, WIN)
    state_f32 = initial_state.astype(jnp.float32)
    extended = extended_2(initial_state, (("lat", 0), ("lon", 1)), half_win)
    field = to_window_order(extended)
    field_f32 = field.astype(jnp.float32)
    field_rms = lax.rsqrt(jnp.mean(field_f32 * field_f32, axis=-1, keepdims=True) + norm_eps)
    normed = (field_f32 * field_rms * norm_gain).astype(jnp.bfloat16)
    flat = jnp.dot(normed.reshape(-1, channels), input_weight, preferred_element_type=jnp.float32)
    proj_windows = flat.astype(jnp.bfloat16).reshape(field.shape[:-1] + (3 * channels,))
    attended = from_window_order(lax.map(band_forward, (proj_windows, valid_bands)))
    attended = attended[half_win : half_win + tile_rows, half_win : half_win + tile_cols].reshape(
        -1, channels
    )
    flat_state = state_f32.reshape(-1, channels)
    block_out = (
        flat_state + jnp.dot(attended, output_weight, preferred_element_type=jnp.float32)
    ).astype(jnp.bfloat16)
    source_dev = foot_tile[:, 0]
    member = (source_dev[:, None] == jnp.arange(devices, dtype=jnp.int32)[None, :]).astype(
        jnp.int32
    )
    bucket_rank = jnp.sum((jnp.cumsum(member, axis=0) - 1) * member, axis=1)
    bucket_slot = source_dev * capacity + bucket_rank
    live_int = (jnp.arange(foot_slots, dtype=jnp.int32) < foot_count[0]).astype(jnp.int32)
    cell_total = tile_rows * tile_cols
    request_buf = jnp.zeros((buffer_rows,), jnp.int32).at[bucket_slot].set(foot_cell)
    asked = lax.all_to_all(request_buf, ("lat", "lon"), split_axis=0, concat_axis=0, tiled=True)
    arrived = lax.all_to_all(
        block_out[asked], ("lat", "lon"), split_axis=0, concat_axis=0, tiled=True
    )
    live = live_int.astype(jnp.float32)
    pre = jnp.dot(arrived[bucket_slot], obs_in_weight, preferred_element_type=jnp.float32)
    sigmoid_pre = jax.nn.sigmoid(pre)
    hidden = (pre * sigmoid_pre).astype(jnp.bfloat16)
    predicted = jnp.dot(hidden, obs_out_weight, preferred_element_type=jnp.float32)
    scaled_res = (predicted - observed.astype(jnp.float32)) / error_scale
    misfit_rows = 0.5 * live * jnp.sum(scaled_res * scaled_res, axis=-1)
    pred_grad = (live[:, None] * scaled_res / error_scale).astype(jnp.bfloat16)
    hidden_grad = jnp.dot(pred_grad, obs_out_weight.T, preferred_element_type=jnp.float32)
    pre_grad = (hidden_grad * sigmoid_pre * (1.0 + pre * (1.0 - sigmoid_pre))).astype(jnp.bfloat16)
    foot_grad = jnp.dot(pre_grad, obs_in_weight.T, preferred_element_type=jnp.float32).astype(
        jnp.bfloat16
    )
    misfit, foot_grad = (misfit_rows, foot_grad)
    grad_buf = jnp.zeros((buffer_rows, channels), jnp.bfloat16).at[bucket_slot].set(foot_grad)
    returned = lax.all_to_all(grad_buf, ("lat", "lon"), split_axis=0, concat_axis=0, tiled=True)
    state_grad = (
        jnp.zeros((cell_total, channels), jnp.float32).at[asked].add(returned.astype(jnp.float32))
    )
    attended_grad = jnp.dot(
        state_grad.astype(jnp.bfloat16), output_weight.T, preferred_element_type=jnp.float32
    ).astype(jnp.bfloat16)
    grad_ext = extended_2(
        attended_grad.reshape(tile_rows, tile_cols, channels), (("lat", 0), ("lon", 1)), half_win
    )
    grad_ext = jnp.where(row_valid[:, None, None], grad_ext, jnp.zeros_like(grad_ext))
    grad_windows = to_window_order(grad_ext)
    proj_grad = from_window_order(lax.map(band_backward, (proj_windows, grad_windows, valid_bands)))
    proj_grad = proj_grad[half_win : half_win + tile_rows, half_win : half_win + tile_cols].reshape(
        -1, 3 * channels
    )
    normed_grad = jnp.dot(proj_grad, input_weight.T, preferred_element_type=jnp.float32)
    scaled = norm_gain * normed_grad
    inv_rms = lax.rsqrt(jnp.mean(flat_state * flat_state, axis=-1, keepdims=True) + norm_eps)
    inner = jnp.mean(flat_state * scaled, axis=-1, keepdims=True)
    gradient = state_grad + inv_rms * scaled - flat_state * inv_rms * inv_rms * inv_rms * inner
    return (gradient.reshape(tile_rows, tile_cols, channels), misfit)


def solution(mesh):
    placed = (
        P("lat", "lon", None),
        P(),
        P(),
        P(),
        P(),
        P(),
        P(("lat", "lon"), None),
        P(),
        P(("lat", "lon"), None),
        P(("lat", "lon")),
        P(("lat", "lon")),
    )
    return jax.shard_map(
        shards,
        mesh=mesh,
        in_specs=placed,
        out_specs=(P("lat", "lon", None), P(("lat", "lon"))),
        check_vma=False,
    )
```

profile of v0, /device:TPU:25, one launch (start us, length us, event | category | flops | bytes accessed | tf_op | source)
XLA Modules:
  0.0 365.9 jit_solution(2787512255973226455)
XLA Ops:
  4.1 2.2 collective-permute-start.1
  9.0 2.6 scatter_custom_fusion
  12.4 9.5 %all-to-all-start = ((s32[128,8,1]{1,2,0:T(1,128)}), s32[128,8,1]{1,2,0:T(1,128)S(1)}, u32[]{:S(2)}, u32[]{:S(2)}) async-start(s32[128,8,1]{1,2,0:T(1,128)} %bitcast.27), calls=%async_computation | async-start | bytes 131072 | tf_op jit(solution)/shard_map/all_to_all | solution.py:151
  21.9 7.8 %all-to-all-done = s32[128,8,1]{1,2,0:T(1,128)S(1)} async-done(((s32[128,8,1]{1,2,0:T(1,128)}), s32[128,8,1]{1,2,0:T(1,128)S(1)}, u32[]{:S(2)}, u32[]{:S(2)}) %all-to-all-start) | async-done | bytes 4128 | tf_op jit(solution)/shard_map/all_to_all | solution.py:151
  32.5 3.4 collective-permute-start.2
  35.9 3.7 %collective-permute-done.2 = bf16[36,6,512]{2,1,0:T(8,128)(2,1)S(1)} collective-permute-done((bf16[36,6,512]{2,1,0:T(8,128)(2,1)S(1)}, bf16[36,6,512]{2,1,0:T(8,128)(2,1)S(1)}, u32[]{:S(2)}, u32[]{:S(2)}) %collective-permute-start.2) | collective-permute-done | bytes 221216 | tf_op jit(solution)/shard_map/ppermute | solution.py:22
  39.6 6.1 %collective-permute-done.3 = bf16[36,6,512]{2,1,0:T(8,128)(2,1)S(1)} collective-permute-done((bf16[36,6,512]{2,1,0:T(8,128)(2,1)S(1)}, bf16[36,6,512]{2,1,0:T(8,128)(2,1)S(1)}, u32[]{:S(2)}, u32[]{:S(2)}) %collective-permute-start.3) | collective-permute-done | bytes 221216 | tf_op jit(solution)/shard_map/ppermute | solution.py:23
  45.7 2.2 maximum_convert_fusion
  47.8 4.4 %reshape.228 = f32[3,12,3,12,512]{4,3,2,1,0:T(8,128)} reshape(f32[36,36,512]{2,1,0:T(8,128)} %maximum_convert_fusion) | data formatting | bytes 5308416 | tf_op jit(solution)/shard_map/convert_element_type | solution.py:129
  52.2 4.5 %copy.82 = f32[3,12,3,12,512]{4,3,1,2,0:T(8,128)} copy(f32[3,12,3,12,512]{4,3,2,1,0:T(8,128)} %reshape.228) | data formatting | bytes 5308416 | tf_op jit(solution)/shard_map/convert_element_type | solution.py:129
  56.7 4.4 %reshape.221 = f32[1296,512]{1,0:T(8,128)} reshape(f32[3,3,12,12,512]{4,3,2,1,0:T(8,128)} %bitcast.170) | data formatting | bytes 5308416 | tf_op jit(solution)/shard_map/convert_element_type | solution.py:129
  62.0 6.0 %convolution_convert_fusion = bf16[1296,1536]{1,0:T(8,128)(2,1)} fusion(bf16[512,1536]{1,0:T(8,128)(2,1)S(1)} %copy-done, f32[1296,512]{1,0:T(8,128)} %reshape.221, f32[512]{0:T(512)S(1)} %copy-done.16, f32[1296]{0:T(1024)S(1)} %rsqrt.23), kind=kOutput, calls=%fused_computation.54 | convolution fusion | flops 2042413056 | bytes 8215616 | tf_op jit(solution)/shard_map/dot_general | solution.py:132
  68.0 8.6 %copy.63 = bf16[3,3,144,1536]{2,3,1,0:T(8,128)(2,1)} copy(bf16[3,3,144,1536]{3,2,1,0:T(8,128)(2,1)} %bitcast.177) | data formatting | bytes 7962624 | tf_op jit(solution)/shard_map/while | solution.py:134
  76.6 33.3 %while.20 = (s32[]{:T(128)}, bf16[3,3,144,512]{3,2,1,0:T(8,128)(2,1)}, bf16[3,3,144,1536]{2,3,1,0:T(8,128)(2,1)}, pred[3,12]{1,0:T(4,128)(4,1)S(1)}, s32[]{:T(128)}) while((s32[]{:T(128)}, bf16[3,3,144,512]{3,2,1,0:T(8,128)(2,1)}, bf16[3,3,144,1536]{2,3,1,0:T(8,128)(2,1)}, pred[3,12]{1,0:T(4,128)(4,1)S(1)}, s32[]{:T(128)}) %tuple.64), condition=%wide.region_8.9_spmd, body=%wide.region_5.8_spmd.sunk | while | flops 130609296 | bytes 12857513 | solution.py:134
  79.7 4.5 %fusion.134 = (f32[3,8,144]{2,1,0:T(8,128)S(1)}, f32[3,8,144,144]{2,3,1,0:T(8,128)}) fusion(pred[144]{0:T(512)(128)(4,1)S(1)} %broadcast_in_dim.132, bf16[3,144,8,64]{1,3,2,0:T(8,128)(2,1)} %bitcast.165, bf16[3,144,8,64]{1,3,2,0:T(8,128)(2,1)S(1)} %bitcast.164), kind=kOutput, calls=%fused_computation.122.clone.1 | convolution fusion | flops 65691792 | bytes 2889360 | tf_op jit(solution)/shard_map/while/body/eval_jaxpr/sub | solution.py:55
  84.3 2.4 fusion.135
  90.8 4.5 %fusion.134 = (f32[3,8,144]{2,1,0:T(8,128)S(1)}, f32[3,8,144,144]{2,3,1,0:T(8,128)}) fusion(pred[144]{0:T(512)(128)(4,1)S(1)} %broadcast_in_dim.132, bf16[3,144,8,64]{1,3,2,0:T(8,128)(2,1)} %bitcast.165, bf16[3,144,8,64]{1,3,2,0:T(8,128)(2,1)S(1)} %bitcast.164), kind=kOutput, calls=%fused_computation.122.clone.1 | convolution fusion | flops 65691792 | bytes 2889360 | tf_op jit(solution)/shard_map/while/body/eval_jaxpr/sub | solution.py:55
  95.4 2.4 fusion.135
  101.9 4.5 %fusion.134 = (f32[3,8,144]{2,1,0:T(8,128)S(1)}, f32[3,8,144,144]{2,3,1,0:T(8,128)}) fusion(pred[144]{0:T(512)(128)(4,1)S(1)} %broadcast_in_dim.132, bf16[3,144,8,64]{1,3,2,0:T(8,128)(2,1)} %bitcast.165, bf16[3,144,8,64]{1,3,2,0:T(8,128)(2,1)S(1)} %bitcast.164), kind=kOutput, calls=%fused_computation.122.clone.1 | convolution fusion | flops 65691792 | bytes 2889360 | tf_op jit(solution)/shard_map/while/body/eval_jaxpr/sub | solution.py:55
  106.5 2.4 fusion.135
  110.0 2.2 reshape.212
  113.7 3.5 reshape.213
  120.1 5.0 %gather_fusion = bf16[1024,512]{1,0:T(8,128)(2,1)} fusion(bf16[576,512]{1,0:T(8,128)(2,1)S(1)} %fusion.51, s32[1024]{0:T(1024)S(1)} %broadcast_clamp_fusion), kind=kCustom, calls=%fused_computation | custom fusion | bytes 2101248 | tf_op jit(solution)/shard_map/gather | solution.py:153
  125.1 6.0 %all-to-all-start.1 = ((bf16[128,8,512]{2,1,0:T(8,128)(2,1)}), bf16[128,8,512]{2,1,0:T(8,128)(2,1)S(1)}, u32[]{:S(2)}, u32[]{:S(2)}) async-start(bf16[128,8,512]{2,1,0:T(8,128)(2,1)} %bitcast.176), calls=%async_computation.1 | async-start | bytes 2097152 | tf_op jit(solution)/shard_map/all_to_all | solution.py:152
  132.0 16.3 %all-to-all-done.1 = bf16[128,8,512]{2,1,0:T(8,128)(2,1)S(1)} async-done(((bf16[128,8,512]{2,1,0:T(8,128)(2,1)}), bf16[128,8,512]{2,1,0:T(8,128)(2,1)S(1)}, u32[]{:S(2)}, u32[]{:S(2)}) %all-to-all-start.1) | async-done | bytes 1048608 | tf_op jit(solution)/shard_map/all_to_all | solution.py:152
  148.3 2.0 gather_fusion.1
  150.3 2.0 fusion.82
  154.7 4.1 %convolution_convert_fusion.2 = bf16[512,512]{1,0:T(8,128)(2,1)} fusion(bf16[512,1024]{1,0:T(8,128)(2,1)S(1)} %copy-done.12, f32[512,1024]{1,0:T(8,128)} %copy-done.11, bf16[1024,256]{1,0:T(8,128)(2,1)S(1)} %copy-done.15, f32[512,256]{0,1:T(8,128)} %get-tuple-element.130, f32[256]{0:T(256)S(1)} %copy-done.18, f32[512]{0:T(512)S(1)} %convert_convert_fusion), kind=kOutput, calls=%fused_computation.72 | convolution fusion | flops 810680320 | bytes 4721664 | tf_op jit(solution)/shard_map/dot_general | solution.py:165
  158.7 4.0 %scatter_custom_fusion.1 = bf16[1024,512]{1,0:T(8,128)(2,1)} fusion(s32[512]{0:T(512)S(1)} %bitcast.189, bf16[512,512]{1,0:T(8,128)(2,1)} %convolution_convert_fusion.2, bf16[]{:T(256)} %constant.59.clone.1), kind=kCustom, calls=%fused_computation.84 | custom fusion | bytes 1049088 | tf_op jit(solution)/shard_map/scatter | solution.py:169
  162.7 7.4 %all-to-all-start.2 = ((bf16[128,8,512]{2,1,0:T(8,128)(2,1)}), bf16[128,8,512]{2,1,0:T(8,128)(2,1)}, u32[]{:S(2)}, u32[]{:S(2)}) async-start(bf16[128,8,512]{2,1,0:T(8,128)(2,1)} %bitcast.38), calls=%async_computation.2 | async-start | bytes 2097152 | tf_op jit(solution)/shard_map/all_to_all | solution.py:170
  170.3 16.6 %all-to-all-done.2 = bf16[128,8,512]{2,1,0:T(8,128)(2,1)} async-done(((bf16[128,8,512]{2,1,0:T(8,128)(2,1)}), bf16[128,8,512]{2,1,0:T(8,128)(2,1)}, u32[]{:S(2)}, u32[]{:S(2)}) %all-to-all-start.2) | async-done | bytes 1048608 | tf_op jit(solution)/shard_map/all_to_all | solution.py:170
  187.0 7.5 %scatter_custom_fusion.2 = f32[576,512]{1,0:T(8,128)S(1)} fusion(s32[1024]{0:T(1024)S(1)} %bitcast.185, bf16[128,8,512]{2,1,0:T(8,128)(2,1)} %all-to-all-done.2, f32[]{:T(128)} %constant.46.clone.1), kind=kCustom, calls=%fused_computation.58 | custom fusion | flops 1048576 | bytes 2228228 | tf_op jit(solution)/shard_map/scatter-add | solution.py:172
  194.5 1.9 convolution_convert_fusion.1
  197.7 3.0 collective-permute-start.5
  200.8 3.2 collective-permute-done.4
  204.0 2.0 collective-permute-done.5
  206.9 4.6 %collective-permute-start.6 = (bf16[36,6,512]{2,1,0:T(8,128)(2,1)S(1)}, bf16[36,6,512]{2,1,0:T(8,128)(2,1)S(1)}, u32[]{:S(2)}, u32[]{:S(2)}) collective-permute-start(bf16[36,6,512]{2,1,0:T(8,128)(2,1)S(1)} %get-tuple-element.117), channel_id=1, source_target_pairs={{0,1},{1,2},{2,3},{3,4},{4,5},{5,6},{6,7},{7,8},{8,9},{9,10},{10,1... | collective-permute-start | bytes 663560 | tf_op jit(solution)/shard_map/ppermute | solution.py:22
  212.1 3.1 collective-permute-done.6
  215.1 6.1 %collective-permute-done.7 = bf16[36,6,512]{2,1,0:T(8,128)(2,1)S(1)} collective-permute-done((bf16[36,6,512]{2,1,0:T(8,128)(2,1)S(1)}, bf16[36,6,512]{2,1,0:T(8,128)(2,1)S(1)}, u32[]{:S(2)}, u32[]{:S(2)}) %collective-permute-start.7) | collective-permute-done | bytes 221216 | tf_op jit(solution)/shard_map/ppermute | solution.py:23
  221.2 2.8 pad_maximum_fusion
  224.1 3.4 concatenate.21
  230.6 110.5 %while.21 = (s32[]{:T(128)}, bf16[3,3,144,1536]{3,2,1,0:T(8,128)(2,1)}, bf16[3,3,144,1536]{2,3,1,0:T(8,128)(2,1)}, pred[3,12]{1,0:T(4,128)(4,1)S(1)}, bf16[3,3,144,512]{3,2,1,0:T(8,128)(2,1)}, /*index=5*/s32[]{:T(128)}) while((s32[]{:T(128)}, bf16[3,3,144,1536]{3,2,1,0:T(8,128)(2,1)}, bf16[3,3,144,1536]{2,3,1,0:T(8,128)(2,1)}, ...), condition=%wide.region_16.17_spmd, body=%wide.region_12.16_spmd.sunk | while | flops 333110464 | bytes 40533284 | solution.py:182
  233.6 4.7 %fusion.147 = (f32[3,8,144]{2,1,0:T(8,128)S(1)}, f32[3,8,144,144]{2,3,1,0:T(8,128)}) fusion(pred[144]{0:T(512)(128)(4,1)S(1)} %broadcast_in_dim.136, bf16[3,144,8,64]{1,3,2,0:T(8,128)(2,1)S(1)} %bitcast.159, bf16[3,144,8,64]{1,3,2,0:T(8,128)(2,1)} %bitcast.161), kind=kOutput, calls=%fused_computation.124.clone.1 | convolution fusion | flops 65691792 | bytes 2889360 | tf_op jit(solution)/shard_map/while/body/eval_jaxpr/sub | solution.py:55
  241.4 2.4 fusion.149
  243.8 7.6 %fusion.151 = bf16[3,8,64,144]{3,2,1,0:T(8,128)(2,1)} fusion(bf16[3,144,8,64]{1,3,2,0:T(8,128)(2,1)} %bitcast.162, f32[3,8,144,144]{2,3,1,0:T(8,128)} %fusion.149, f32[3,8,144,144]{2,3,1,0:T(8,128)} %get-tuple-element.204, f32[3,8,144]{2,1,0:T(8,128)S(1)} %get-tuple-element.205), kind=kOutput, calls=%fused_computation.42.clone.1 | convolution fusion | flops 67409424 | bytes 4879872 | tf_op jit(solution)/shard_map/while/body/eval_jaxpr/nhqk,nkhe->nqhe/dot_general | solution.py:86
  251.4 7.3 %fusion.150 = bf16[3,8,64,144]{3,2,1,0:T(8,128)(2,1)} fusion(bf16[3,144,8,64]{1,3,2,0:T(8,128)(2,1)S(1)} %bitcast.160, f32[3,8,144,144]{2,3,1,0:T(8,128)} %fusion.149, f32[3,8,144,144]{2,3,1,0:T(8,128)} %get-tuple-element.204, f32[3,8,144]{2,1,0:T(8,128)S(1)} %get-tuple-element.205), kind=kOutput, calls=%fused_computation.43.clone.1 | convolution fusion | flops 67409424 | bytes 4879872 | tf_op jit(solution)/shard_map/while/body/eval_jaxpr/nhqk,nqhe->nkhe/dot_general | solution.py:87
  258.7 2.8 fusion.148
  263.5 2.7 copy.88
  270.4 4.7 %fusion.147 = (f32[3,8,144]{2,1,0:T(8,128)S(1)}, f32[3,8,144,144]{2,3,1,0:T(8,128)}) fusion(pred[144]{0:T(512)(128)(4,1)S(1)} %broadcast_in_dim.136, bf16[3,144,8,64]{1,3,2,0:T(8,128)(2,1)S(1)} %bitcast.159, bf16[3,144,8,64]{1,3,2,0:T(8,128)(2,1)} %bitcast.161), kind=kOutput, calls=%fused_computation.124.clone.1 | convolution fusion | flops 65691792 | bytes 2889360 | tf_op jit(solution)/shard_map/while/body/eval_jaxpr/sub | solution.py:55
  278.2 2.4 fusion.149
  280.7 7.6 %fusion.151 = bf16[3,8,64,144]{3,2,1,0:T(8,128)(2,1)} fusion(bf16[3,144,8,64]{1,3,2,0:T(8,128)(2,1)} %bitcast.162, f32[3,8,144,144]{2,3,1,0:T(8,128)} %fusion.149, f32[3,8,144,144]{2,3,1,0:T(8,128)} %get-tuple-element.204, f32[3,8,144]{2,1,0:T(8,128)S(1)} %get-tuple-element.205), kind=kOutput, calls=%fused_computation.42.clone.1 | convolution fusion | flops 67409424 | bytes 4879872 | tf_op jit(solution)/shard_map/while/body/eval_jaxpr/nhqk,nkhe->nqhe/dot_general | solution.py:86
  288.2 7.3 %fusion.150 = bf16[3,8,64,144]{3,2,1,0:T(8,128)(2,1)} fusion(bf16[3,144,8,64]{1,3,2,0:T(8,128)(2,1)S(1)} %bitcast.160, f32[3,8,144,144]{2,3,1,0:T(8,128)} %fusion.149, f32[3,8,144,144]{2,3,1,0:T(8,128)} %get-tuple-element.204, f32[3,8,144]{2,1,0:T(8,128)S(1)} %get-tuple-element.205), kind=kOutput, calls=%fused_computation.43.clone.1 | convolution fusion | flops 67409424 | bytes 4879872 | tf_op jit(solution)/shard_map/while/body/eval_jaxpr/nhqk,nqhe->nkhe/dot_general | solution.py:87
  295.5 2.8 fusion.148
  300.3 2.7 copy.88
  307.3 4.7 %fusion.147 = (f32[3,8,144]{2,1,0:T(8,128)S(1)}, f32[3,8,144,144]{2,3,1,0:T(8,128)}) fusion(pred[144]{0:T(512)(128)(4,1)S(1)} %broadcast_in_dim.136, bf16[3,144,8,64]{1,3,2,0:T(8,128)(2,1)S(1)} %bitcast.159, bf16[3,144,8,64]{1,3,2,0:T(8,128)(2,1)} %bitcast.161), kind=kOutput, calls=%fused_computation.124.clone.1 | convolution fusion | flops 65691792 | bytes 2889360 | tf_op jit(solution)/shard_map/while/body/eval_jaxpr/sub | solution.py:55
  315.1 2.4 fusion.149
  317.5 7.6 %fusion.151 = bf16[3,8,64,144]{3,2,1,0:T(8,128)(2,1)} fusion(bf16[3,144,8,64]{1,3,2,0:T(8,128)(2,1)} %bitcast.162, f32[3,8,144,144]{2,3,1,0:T(8,128)} %fusion.149, f32[3,8,144,144]{2,3,1,0:T(8,128)} %get-tuple-element.204, f32[3,8,144]{2,1,0:T(8,128)S(1)} %get-tuple-element.205), kind=kOutput, calls=%fused_computation.42.clone.1 | convolution fusion | flops 67409424 | bytes 4879872 | tf_op jit(solution)/shard_map/while/body/eval_jaxpr/nhqk,nkhe->nqhe/dot_general | solution.py:86
  325.1 7.3 %fusion.150 = bf16[3,8,64,144]{3,2,1,0:T(8,128)(2,1)} fusion(bf16[3,144,8,64]{1,3,2,0:T(8,128)(2,1)S(1)} %bitcast.160, f32[3,8,144,144]{2,3,1,0:T(8,128)} %fusion.149, f32[3,8,144,144]{2,3,1,0:T(8,128)} %get-tuple-element.204, f32[3,8,144]{2,1,0:T(8,128)S(1)} %get-tuple-element.205), kind=kOutput, calls=%fused_computation.43.clone.1 | convolution fusion | flops 67409424 | bytes 4879872 | tf_op jit(solution)/shard_map/while/body/eval_jaxpr/nhqk,nqhe->nkhe/dot_general | solution.py:87
  332.4 2.8 fusion.148
  337.2 2.7 copy.88
  341.1 7.0 %reshape.217 = bf16[3,3,12,12,1536]{4,3,2,1,0:T(8,128)(2,1)} reshape(bf16[3,3,144,1536]{3,2,1,0:T(8,128)(2,1)} %get-tuple-element.52) | data formatting | bytes 7962624 | tf_op jit(solution)/shard_map/reshape | solution.py:38
  348.1 5.2 %copy.71 = bf16[3,12,3,12,1536]{4,3,2,1,0:T(8,128)(2,1)} copy(bf16[3,12,3,12,1536]{4,3,1,2,0:T(8,128)(2,1)} %bitcast.158) | data formatting | bytes 7962624 | tf_op jit(solution)/shard_map/transpose | solution.py:38
  353.3 7.6 %reshape.218 = bf16[36,36,1536]{2,1,0:T(8,128)(2,1)} reshape(bf16[3,12,3,12,1536]{4,3,2,1,0:T(8,128)(2,1)} %copy.71) | data formatting | bytes 7962624 | tf_op jit(solution)/shard_map/reshape | solution.py:39
  360.9 2.4 slice.90
  (155 shorter events, 66.2 us)
Async XLA Ops:
  0.6 61.3 %copy-start = (bf16[512,1536]{1,0:T(8,128)(2,1)S(1)}, bf16[512,1536]{1,0:T(8,128)(2,1)}, u32[]{:S(2)}) copy-start(bf16[512,1536]{1,0:T(8,128)(2,1)} %param.17) | copy-start | bytes 4718596
  0.6 30.5 %copy-start.9 = (bf16[24,24,512]{2,1,0:T(8,128)(2,1)S(1)}, bf16[24,24,512]{2,1,0:T(8,128)(2,1)}, u32[]{:S(2)}) copy-start(bf16[24,24,512]{2,1,0:T(8,128)(2,1)} %param.15) | copy-start | bytes 1769476
  2.5 28.6 %collective-permute-start = (bf16[6,24,512]{2,1,0:T(8,128)(2,1)}, bf16[6,24,512]{2,1,0:T(8,128)(2,1)S(1)}, u32[]{:S(2)}, u32[]{:S(2)}) collective-permute-start(bf16[6,24,512]{2,1,0:T(8,128)(2,1)} %get-tuple-element.124), channel_id=1, source_target_pairs={{0,16},{16,32},{32,48},{48,64},{64,80},{80,96},{96,112},{112,0},{1... | collective-permute-start | bytes 442376 | tf_op jit(solution)/shard_map/ppermute | solution.py:22
  4.1 28.3 %collective-permute-start.1 = (bf16[6,24,512]{2,1,0:T(8,128)(2,1)S(1)}, bf16[6,24,512]{2,1,0:T(8,128)(2,1)S(1)}, u32[]{:S(2)}, u32[]{:S(2)}) collective-permute-start(bf16[6,24,512]{2,1,0:T(8,128)(2,1)S(1)} %get-tuple-element.123), channel_id=1, source_target_pairs={{16,0},{32,16},{48,32},{64,48},{80,64},{96,80},{112,96},{0,112},{1... | collective-permute-start | bytes 442376 | tf_op jit(solution)/shard_map/ppermute | solution.py:23
  12.4 17.3 %all-to-all-start = ((s32[128,8,1]{1,2,0:T(1,128)}), s32[128,8,1]{1,2,0:T(1,128)S(1)}, u32[]{:S(2)}, u32[]{:S(2)}) async-start(s32[128,8,1]{1,2,0:T(1,128)} %bitcast.27), calls=%async_computation | async-start | bytes 131072 | tf_op jit(solution)/shard_map/all_to_all | solution.py:151
  32.5 7.1 %collective-permute-start.2 = (bf16[36,6,512]{2,1,0:T(8,128)(2,1)S(1)}, bf16[36,6,512]{2,1,0:T(8,128)(2,1)S(1)}, u32[]{:S(2)}, u32[]{:S(2)}) collective-permute-start(bf16[36,6,512]{2,1,0:T(8,128)(2,1)S(1)} %get-tuple-element.119), channel_id=1, source_target_pairs={{0,1},{1,2},{2,3},{3,4},{4,5},{5,6},{6,7},{7,8},{8,9},{9,10},{10,1... | collective-permute-start | bytes 663560 | tf_op jit(solution)/shard_map/ppermute | solution.py:22
  35.9 9.8 %collective-permute-start.3 = (bf16[36,6,512]{2,1,0:T(8,128)(2,1)S(1)}, bf16[36,6,512]{2,1,0:T(8,128)(2,1)S(1)}, u32[]{:S(2)}, u32[]{:S(2)}) collective-permute-start(bf16[36,6,512]{2,1,0:T(8,128)(2,1)S(1)} %get-tuple-element.120), channel_id=1, source_target_pairs={{1,0},{2,1},{3,2},{4,3},{5,4},{6,5},{7,6},{8,7},{9,8},{10,9},{11,1... | collective-permute-start | bytes 663560 | tf_op jit(solution)/shard_map/ppermute | solution.py:23
  56.7 5.3 %copy-start.16 = (f32[512]{0:T(512)S(1)}, f32[512]{0:T(512)}, u32[]{:S(2)}) copy-start(f32[512]{0:T(512)} %param.16) | copy-start | bytes 6148
  113.7 4.9 %copy-start.5 = (f32[24,24,512]{2,1,0:T(8,128)S(1)}, f32[24,24,512]{2,1,0:T(8,128)}, u32[]{:S(2)}) copy-start(f32[24,24,512]{2,1,0:T(8,128)} %get-tuple-element.126) | copy-start | bytes 3538948
  120.1 11.1 %copy-start.13 = (bf16[512,256]{1,0:T(8,128)(2,1)S(1)}, bf16[512,256]{1,0:T(8,128)(2,1)}, u32[]{:S(2)}) copy-start(bf16[512,256]{1,0:T(8,128)(2,1)} %param.21) | copy-start | bytes 786436
  125.1 23.2 %all-to-all-start.1 = ((bf16[128,8,512]{2,1,0:T(8,128)(2,1)}), bf16[128,8,512]{2,1,0:T(8,128)(2,1)S(1)}, u32[]{:S(2)}, u32[]{:S(2)}) async-start(bf16[128,8,512]{2,1,0:T(8,128)(2,1)} %bitcast.176), calls=%async_computation.1 | async-start | bytes 2097152 | tf_op jit(solution)/shard_map/all_to_all | solution.py:152
  150.3 2.0 copy-start.14
  150.3 2.0 copy-start.18
  152.4 1.7 copy-start.11
  152.4 2.0 copy-start.12
  152.4 2.3 copy-start.15
  158.7 11.4 %copy-start.10 = (bf16[24,24,512]{2,1,0:T(8,128)(2,1)S(1)}, bf16[24,24,512]{2,1,0:T(8,128)(2,1)}, u32[]{:S(2)}) copy-start(bf16[24,24,512]{2,1,0:T(8,128)(2,1)} %param.15) | copy-start | bytes 1769476
  162.7 24.2 %all-to-all-start.2 = ((bf16[128,8,512]{2,1,0:T(8,128)(2,1)}), bf16[128,8,512]{2,1,0:T(8,128)(2,1)}, u32[]{:S(2)}, u32[]{:S(2)}) async-start(bf16[128,8,512]{2,1,0:T(8,128)(2,1)} %bitcast.38), calls=%async_computation.2 | async-start | bytes 2097152 | tf_op jit(solution)/shard_map/all_to_all | solution.py:170
  194.4 29.6 %copy-start.7 = (f32[576,512]{1,0:T(8,128)}, f32[576,512]{1,0:T(8,128)S(1)}, u32[]{:S(2)}) copy-start(f32[576,512]{1,0:T(8,128)S(1)} %scatter_custom_fusion.2) | copy-start | bytes 3538948
  197.1 6.9 %collective-permute-start.4 = (bf16[6,24,512]{2,1,0:T(8,128)(2,1)}, bf16[6,24,512]{2,1,0:T(8,128)(2,1)S(1)}, u32[]{:S(2)}, u32[]{:S(2)}) collective-permute-start(bf16[6,24,512]{2,1,0:T(8,128)(2,1)} %bitcast.40), channel_id=1, source_target_pairs={{0,16},{16,32},{32,48},{48,64},{64,80},{80,96},{96,112},{112,0},{1... | collective-permute-start | bytes 442376 | tf_op jit(solution)/shard_map/ppermute | solution.py:22
  197.7 8.3 %collective-permute-start.5 = (bf16[6,24,512]{2,1,0:T(8,128)(2,1)}, bf16[6,24,512]{2,1,0:T(8,128)(2,1)}, u32[]{:S(2)}, u32[]{:S(2)}) collective-permute-start(bf16[6,24,512]{2,1,0:T(8,128)(2,1)} %bitcast.42), channel_id=1, source_target_pairs={{16,0},{32,16},{48,32},{64,48},{80,64},{96,80},{112,96},{0,112},{1... | collective-permute-start | bytes 442376 | tf_op jit(solution)/shard_map/ppermute | solution.py:23
  206.9 8.2 %collective-permute-start.6 = (bf16[36,6,512]{2,1,0:T(8,128)(2,1)S(1)}, bf16[36,6,512]{2,1,0:T(8,128)(2,1)S(1)}, u32[]{:S(2)}, u32[]{:S(2)}) collective-permute-start(bf16[36,6,512]{2,1,0:T(8,128)(2,1)S(1)} %get-tuple-element.117), channel_id=1, source_target_pairs={{0,1},{1,2},{2,3},{3,4},{4,5},{5,6},{6,7},{7,8},{8,9},{9,10},{10,1... | collective-permute-start | bytes 663560 | tf_op jit(solution)/shard_map/ppermute | solution.py:22
  211.5 9.8 %collective-permute-start.7 = (bf16[36,6,512]{2,1,0:T(8,128)(2,1)S(1)}, bf16[36,6,512]{2,1,0:T(8,128)(2,1)S(1)}, u32[]{:S(2)}, u32[]{:S(2)}) collective-permute-start(bf16[36,6,512]{2,1,0:T(8,128)(2,1)S(1)} %get-tuple-element.118), channel_id=1, source_target_pairs={{1,0},{2,1},{3,2},{4,3},{5,4},{6,5},{7,6},{8,7},{9,8},{10,9},{11,1... | collective-permute-start | bytes 663560 | tf_op jit(solution)/shard_map/ppermute | solution.py:23
  233.4 4.9 %copy-start.1 = (bf16[3,144,512]{1,2,0:T(8,128)(2,1)}, bf16[3,144,512]{1,2,0:T(8,128)(2,1)S(1)}, u32[]{:S(2)}) copy-start(bf16[3,144,512]{1,2,0:T(8,128)(2,1)S(1)} %get-tuple-element.202) | copy-start | bytes 1327108 | tf_op jit(solution)/shard_map/while
  243.8 7.6 %copy-start.2 = (bf16[3,144,512]{1,2,0:T(8,128)(2,1)S(1)}, bf16[3,144,512]{1,2,0:T(8,128)(2,1)}, u32[]{:S(2)}) copy-start(bf16[3,144,512]{1,2,0:T(8,128)(2,1)} %copy-done.1) | copy-start | bytes 1327108 | tf_op jit(solution)/shard_map/while
  258.7 2.8 copy-start.3
  258.7 2.9 copy-start.4
  270.2 4.9 %copy-start.1 = (bf16[3,144,512]{1,2,0:T(8,128)(2,1)}, bf16[3,144,512]{1,2,0:T(8,128)(2,1)S(1)}, u32[]{:S(2)}) copy-start(bf16[3,144,512]{1,2,0:T(8,128)(2,1)S(1)} %get-tuple-element.202) | copy-start | bytes 1327108 | tf_op jit(solution)/shard_map/while
  280.6 7.6 %copy-start.2 = (bf16[3,144,512]{1,2,0:T(8,128)(2,1)S(1)}, bf16[3,144,512]{1,2,0:T(8,128)(2,1)}, u32[]{:S(2)}) copy-start(bf16[3,144,512]{1,2,0:T(8,128)(2,1)} %copy-done.1) | copy-start | bytes 1327108 | tf_op jit(solution)/shard_map/while
  295.5 2.8 copy-start.3
  295.5 2.9 copy-start.4
  307.1 4.9 %copy-start.1 = (bf16[3,144,512]{1,2,0:T(8,128)(2,1)}, bf16[3,144,512]{1,2,0:T(8,128)(2,1)S(1)}, u32[]{:S(2)}) copy-start(bf16[3,144,512]{1,2,0:T(8,128)(2,1)S(1)} %get-tuple-element.202) | copy-start | bytes 1327108 | tf_op jit(solution)/shard_map/while
  317.5 7.6 %copy-start.2 = (bf16[3,144,512]{1,2,0:T(8,128)(2,1)S(1)}, bf16[3,144,512]{1,2,0:T(8,128)(2,1)}, u32[]{:S(2)}) copy-start(bf16[3,144,512]{1,2,0:T(8,128)(2,1)} %copy-done.1) | copy-start | bytes 1327108 | tf_op jit(solution)/shard_map/while
  332.4 2.8 copy-start.3
  332.4 2.9 copy-start.4
  360.9 2.4 copy-start.6
  360.9 2.4 copy-start.17
  363.3 1.3 copy-start.8
where the time goes:
time: 369 us; the launch traced here: 366 us
  local copies, waits for them, and re-layouts  120 us (33%)
  matrix products  114 us (31%)
  waiting for transfers between devices  64.8 us (18%)
  starting transfers between devices  38.4 us (10%)
  other arithmetic  27.5 us (7%)
    sub x6, matrix products, softmax_weights(): expo = jnp.exp(scores - top)  27.7 us
    dot_general x3, matrix products, band_backward(): jnp.einsum('nhqk,nkhe->nqhe', score_grad, keys, preferred_element_type=jn...  22.7 us
    dot_general x3, matrix products, band_backward(): jnp.einsum('nhqk,nqhe->nkhe', score_grad, queries, preferred_element_type...  21.9 us
    all_to_all x1, waiting for transfers between devices, shards(): lax.all_to_all(grad_buf, ('lat', 'lon'), split_axis=0, concat_axis=0, til...  16.6 us
    all_to_all x1, waiting for transfers between devices, shards(): lax.all_to_all(block_out[asked], ('lat', 'lon'), split_axis=0, concat_axi...  16.3 us
    ppermute x4, waiting for transfers between devices, extended_2(): after = lax.ppermute(first, axis, down)  14.2 us
    convert_element_type x3, local copies, waits for them, and re-layouts, shards(): field_f32 = field.astype(jnp.float32)  13.2 us
    dynamic_update_slice x6, local copies, waits for them, and re-layouts, shards(): lax.map(band_backward, (proj_windows, grad_windows, valid_bands))  11.8 us
  transfers between devices with their start and end apart: 11, of which 9 were waited for; matrix products, arithmetic and copies ran while one was open for 2% of the time, Pallas kernels for 0%

commit v1 on v0

v1 whole, which is shorter than its diff:
```python
import functools

import jax
import jax.numpy as jnp
import numpy as np
from jax import lax
from jax.experimental import pallas as pl
from jax.experimental.pallas import tpu as pltpu
from jax.sharding import PartitionSpec as P

HEADS = 8
WIN = 12
HALF = WIN // 2
SIDE = 2 * WIN
CELLS = SIDE * SIDE
AREA = WIN * WIN
STRIP = HALF * SIDE
MAIN = 128
LATE = AREA - MAIN
SRC = 384
NORM_EPS = 1e-06
MESH = pl.DeviceIdType.MESH
BF = jnp.bfloat16
F32 = jnp.float32

WINDOWS = ((1, 0), (0, 1), (0, 0), (1, 1))
REACH = 3 * STRIP
ACROSS = SIDE - HALF
SIDES, CORNER = 112, 48
LEFT, TOP, TL = 0, SIDES, 2 * SIDES
MARGIN = 2 * SIDES + CORNER
PIECES = ((LEFT, SIDES, 0, 1), (TOP, SIDES, 1, 0), (TL, CORNER, 1, 1))
SOURCES = (
    ((True, 144, 288), (False, LEFT + 32, 80), (True, 0, 16)),
    ((True, 0, 272), (False, TOP, SIDES)),
    ((True, 0, 176), (False, TOP, SIDES), (False, LEFT, 48), (False, TL, CORNER)),
    ((True, 144, 288), (True, 0, 96)),
)
TARGETS = (
    (0, STRIP, (1, 2)),
    (STRIP, 2 * STRIP, (0, 3)),
    (REACH + LEFT, SIDES, (0, 2)),
    (REACH + TOP, SIDES, (1, 2)),
    (REACH + TL, CORNER, (2,)),
)


def place_of(row, col):
    if row >= 0 and col >= 0:
        return True, row * SIDE + col
    if col >= 0:
        return False, TOP + (row + HALF) * ACROSS + col
    if row >= 0:
        return False, LEFT + row * HALF + col + HALF
    return False, TL + (row + HALF) * HALF + col + HALF


def selectors():
    pack = np.zeros((MARGIN, CELLS), np.float32)
    for a in range(HALF):
        for b in range(ACROSS):
            pack[LEFT + b * HALF + a, b * SIDE + ACROSS + a] = 1
            pack[TOP + a * ACROSS + b, (ACROSS + a) * SIDE + b] = 1
        for b in range(HALF):
            pack[TL + a * HALF + b, (ACROSS + a) * SIDE + ACROSS + b] = 1
    gather = np.zeros((4, AREA, SRC), np.float32)
    spread = np.zeros((4, REACH + MARGIN, AREA), np.float32)
    spread_q = np.zeros((4, REACH + MARGIN, 2 * MAIN), np.float32)
    for w, (i, j) in enumerate(WINDOWS):
        where = {}
        at = 0
        for own, first, rows in SOURCES[w]:
            for row in range(rows):
                where.setdefault((own, first + row), at + row)
            at += rows
        for a in range(WIN):
            for b in range(WIN):
                own, spot = place_of(WIN * i - HALF + a, WIN * j - HALF + b)
                cell = a * WIN + b
                gather[w, cell, where[own, spot]] = 1
                to = spot if own else REACH + spot
                spread[w, to, cell] = 1
                for h in range(HEADS if cell >= MAIN else 1):
                    spread_q[w, to, cell + h * LATE] = 1
    return pack, gather, spread, spread_q


def nn(a, b):
    return jnp.dot(a, b, preferred_element_type=F32)


def nt(a, b):
    return lax.dot_general(a, b, (((1,), (1,)), ((), ())), preferred_element_type=F32)


def iota(shape, dim):
    return lax.broadcasted_iota(jnp.int32, shape, dim)


def normalize(x_ref, gain, into):
    step = 48 if x_ref.shape[0] % 48 == 0 else 16
    for first in range(0, x_ref.shape[0], step):
        here = pl.ds(first, step)
        x = x_ref[here, :].astype(F32)
        rms = lax.rsqrt(jnp.mean(x * x, axis=-1, keepdims=True) + NORM_EPS)
        into[here, :] = (x * rms * gain).astype(BF)


def each(first, last, act):
    def one(step, carry):
        act(step)
        return carry

    lax.fori_loop(first, last, one, 0)


def start(copies):
    for copy in copies:
        copy.start()


def wait(copies):
    for copy in copies:
        copy.wait()


class Links:
    def __init__(self, lats, lons, margin_sem, foot_sem, line_sem):
        self.lats, self.lons, self.n = lats, lons, lats * lons
        self.lat, self.lon = lax.axis_index("lat"), lax.axis_index("lon")
        self.margin_sem, self.foot_sem, self.line_sem = margin_sem, foot_sem, line_sem
        self.barrier = pltpu.get_barrier_semaphore()

    def around(self, up, right):
        lats, lons = self.lats, self.lons
        return lax.rem(self.lat + up + lats, lats), lax.rem(self.lon + right + lons, lons)

    def away_by(self, d):
        return self.around(d // self.lons, d % self.lons)

    def signal(self, sem, device):
        pl.semaphore_signal(sem, inc=1, device_id=device, device_id_type=MESH)

    def greet(self):
        for step in range(1, self.lats):
            self.signal(self.barrier, self.around(step, 0))
        for step in range(1, self.lons):
            self.signal(self.barrier, self.around(0, step))

    def met(self):
        pl.semaphore_wait(self.barrier, self.lats - 1 + self.lons - 1)
        for step in range(1, self.lats):
            self.signal(self.line_sem, self.around(step, 0))
        pl.semaphore_wait(self.line_sem, self.lats - 1)

    def copy(self, sems, i, src, dst, device):
        return pltpu.make_async_remote_copy(
            src_ref=src,
            dst_ref=dst,
            send_sem=sems.at[2 * i],
            recv_sem=sems.at[2 * i + 1],
            device_id=device,
            device_id_type=MESH,
        )

    def pieces(self, base, src, into, way):
        return [
            self.copy(
                self.margin_sem,
                base + i,
                src.at[pl.ds(first, rows)],
                into.at[pl.ds(first, rows)],
                self.around(way * up, way * right),
            )
            for i, (first, rows, up, right) in enumerate(PIECES)
        ]

    def arrived(self, into, i, parts):
        rest = into.at[pl.ds(1, parts - 1)]
        self.copy(self.foot_sem, i, rest, rest, self.around(1, 0)).wait()

    def to_all(self, send, into, i):
        def one(d):
            self.copy(self.foot_sem, i, send.at[d], into.at[d], self.away_by(d)).start()

        steps = (self.n - 1) // 7

        def seven(k, carry):
            for j in range(7):
                one(1 + 7 * k + j)
            return carry

        lax.fori_loop(0, steps, seven, 0)
        for d in range(1 + 7 * steps, self.n):
            one(d)
        into[0] = send[0]

    def along_lon(self, send, into, i, way):
        for step in range(1, self.lons):
            device = self.around(0, way * step)
            self.copy(self.foot_sem, i, send.at[:, step], into.at[step], device).start()
        into[0] = send[:, 0]

    def along_lat(self, send, into, i, way):
        for step in range(1, self.lats):
            device = self.around(way * step, 0)
            self.copy(self.foot_sem, i, send.at[:, step], into.at[step], device).start()
        into[0] = send[:, 0]


def footprint_places(links, tile_id, count, cap):
    lats, lons, n = links.lats, links.lons, links.n
    feet = tile_id.shape[1]
    tile_lat = jnp.floor((tile_id[...].astype(F32) + 0.5) * (1.0 / lons)).astype(jnp.int32)
    up, right = tile_lat - links.lat, tile_id[...] - tile_lat * lons - links.lon
    up, right = jnp.where(up < 0, up + lats, up), jnp.where(right < 0, right + lons, right)
    away = up * lons + right
    live = iota((1, feet), 1) < count[...]
    named = (iota((n, feet), 0) == away).astype(F32)
    before = (iota((feet, feet), 0) < iota((feet, feet), 1)).astype(F32).astype(BF)
    rank = jnp.sum(nn(named.astype(BF), before) * named, axis=0, keepdims=True).astype(jnp.int32)
    return away, rank, live, named


class Heads:
    def __init__(self, chans):
        self.even = (iota((1, 128), 1) < 64).astype(F32).astype(BF)
        self.odd = (iota((1, 128), 1) >= 64).astype(F32).astype(BF)
        self.eye = (iota((128, 128), 0) == iota((128, 128), 1)).astype(F32).astype(BF)
        late_head = iota((MAIN, chans), 0) >> 4 == iota((MAIN, chans), 1) >> 6
        self.late_head = late_head.astype(F32).astype(BF)
        head_late = iota((chans, MAIN), 0) >> 6 == iota((chans, MAIN), 1) >> 4
        self.head_late = head_late.astype(F32)

    def stacked(self, x):
        return jnp.concatenate([x * self.even, x * self.odd], axis=0)

    def late_rows(self, x):
        return jnp.concatenate([x] * HEADS, axis=0) * self.late_head

    def turned(self, qkv, w, first):
        return [
            nt(self.eye, pair_of(qkv, w, first, AREA, pair)).astype(BF)
            for pair in range(HEADS // 2)
        ]


def pair_of(ref, w, first, rows, pair):
    return ref[w, 0:rows, first + 128 * pair : first + 128 * (pair + 1)]


def gather_window(source, w, tile_ref, margin_ref):
    at = 0
    for own, first, count_rows in SOURCES[w]:
        piece = (tile_ref if own else margin_ref)[pl.ds(first, count_rows), :]
        source[w, pl.ds(at, count_rows), :] = piece
        at += count_rows


RETURNED = tuple(
    [(SIDE * row + ACROSS, HALF, LEFT + HALF * row) for row in range(ACROSS)]
    + [(REACH + SIDE * row, ACROSS, TOP + ACROSS * row) for row in range(HALF)]
    + [(REACH + SIDE * row + ACROSS, HALF, TL + HALF * row) for row in range(HALF)]
)


def to_targets(selector, per_window, which):
    first, count_rows, windows = TARGETS[which]
    total = None
    for w in windows:
        part = per_window(selector[w, pl.ds(first, count_rows), :], w)
        total = part if total is None else total + part
    return total


def kernel(
    lats,
    lons,
    cap,
    state_hbm,
    gain,
    w_in_hbm,
    w_out_hbm,
    obs_in_hbm,
    obs_out_hbm,
    observed_hbm,
    scale,
    tile_id,
    cell_id,
    count,
    pack_hbm,
    gather_hbm,
    spread_hbm,
    spread_q_hbm,
    own_part_hbm,
    back_part_hbm,
    misfit,
    state,
    observed,
    pack_m,
    w_in,
    w_out,
    obs_in,
    obs_out,
    gather_m,
    spread_m,
    spread_q_m,
    packed,
    margin,
    own_n,
    margin_n,
    source,
    win,
    qkv,
    apart,
    probs,
    att_t,
    att_send,
    att_recv,
    attended,
    block_out,
    obs_send,
    obs_recv,
    idx_send,
    idx_mid,
    idx_recv,
    mis_send,
    mis_mid,
    mis_recv,
    chosen,
    silu_grad,
    hidden,
    predicted,
    residuals,
    foot_grad,
    onehot,
    back,
    back_packed,
    state_grad,
    att_grad,
    packed_g,
    margin_g,
    dk_w,
    dv_w,
    dq_t,
    proj_grad,
    part_send,
    part_recv,
    own_part,
    margin_sem,
    foot_sem,
    fetch_sem,
    store_sem,
    line_sem,
):
    links = Links(lats, lons, margin_sem, foot_sem, line_sem)
    links.greet()
    n = links.n
    slots = n * cap
    feet = tile_id.shape[1]
    chans = state.shape[1]
    fetches = [
        pltpu.make_async_copy(src, dst, fetch_sem.at[i])
        for i, (src, dst) in enumerate(
            (
                (gather_hbm, gather_m),
                (w_in_hbm, w_in),
                (spread_q_hbm, spread_q_m),
                (w_out_hbm, w_out),
                (obs_in_hbm, obs_in),
                (obs_out_hbm, obs_out),
                (spread_hbm, spread_m),
                (state_hbm, state),
                (pack_hbm, pack_m),
                (observed_hbm, observed),
            )
        )
    ]
    start(fetches[7:])
    start(fetches[:7])
    fetches[7].wait()
    fetches[8].wait()

    packed[...] = nn(pack_m[...], state[...]).astype(BF)

    links.met()
    state_copies = links.pieces(0, packed, margin, 1)
    start(state_copies)

    away, rank, live, named = footprint_places(links, tile_id, count, cap)
    slot = jnp.where(live, away * cap + rank, -1)
    cell_value = (cell_id[...] + 1).astype(F32)
    on_lane = iota((4, cap, 128), 2) == iota((4, cap, 128), 1)
    cells = []
    for first in range(0, slots, 4 * cap):
        block = (iota((4 * cap, feet), 0) + first == slot).astype(F32)
        chosen[pl.ds(first, 4 * cap), :] = block.astype(BF)
        cell = jnp.sum(block * cell_value, axis=1, keepdims=True) - 1.0
        cell = jnp.where(on_lane, cell.reshape(4, cap, 1), 0.0)
        cells.append(jnp.sum(cell, axis=1, keepdims=True))
    idx_send[...] = jnp.concatenate(cells, axis=0).reshape(lats, lons, 1, 128)
    links.along_lon(idx_send, idx_mid, 0, 1)
    fetches[9].wait()
    rows = nn(chosen[...], observed[...])
    half = rows.shape[1] // 2
    rows = rows.reshape(n, cap, 2 * half)
    obs_send[...] = jnp.concatenate([rows[:, :, :half], rows[:, :, half:]], axis=1).astype(BF)

    links.to_all(obs_send, obs_recv, 1)

    normalize(state, gain[...], own_n)

    def place(windows):
        for w in windows:
            win[w] = nn(gather_m[w], source[w]).astype(BF)

    def project(first, last):
        cells = win[first:last].reshape((last - first) * AREA, chans)
        for part in range(3):
            cols = slice(part * chans, (part + 1) * chans)
            out = nn(cells, w_in[:, cols])
            out = (out * 0.125 if part == 0 else out).astype(BF)
            qkv[first:last, :, cols] = out.reshape(last - first, AREA, chans)

    heads = Heads(chans)

    def softmax(scores):
        e = jnp.exp(scores - jnp.max(scores, axis=0, keepdims=True))
        return e * (1.0 / jnp.sum(e, axis=0, keepdims=True))

    def forward(w):
        row = jnp.where((w == 1) | (w == 2), 0, 1)
        late = heads.late_rows(qkv[w, MAIN:AREA, 0:chans])
        values_t = heads.turned(qkv, w, 2 * chans)

        def scored(pair):
            if pair < HEADS // 2:
                queries = heads.stacked(pair_of(qkv, w, 0, MAIN, pair))
                return nt(pair_of(qkv, w, chans, AREA, pair), queries)
            return nt(qkv[w, :, chans : 2 * chans], late)

        after = scored(0)
        for pair in range(HEADS // 2):
            scores, after = after, scored(pair + 1)
            for h in range(2):
                lanes = slice(MAIN * h, MAIN * (h + 1))
                p = softmax(scores[:, lanes] + apart[row, :, lanes])
                probs[w, :, 256 * pair + MAIN * h : 256 * pair + MAIN * (h + 1)] = p
                at = 128 * pair + 64 * h
                out = nn(values_t[pair][64 * h : 64 * h + 64], p.astype(BF))
                att_t[w, at : at + 64, 0:MAIN] = out.astype(BF)
        p = softmax(after + apart[row, :, 2 * MAIN :])
        probs[w, :, MAIN * HEADS :] = p
        out = nn(jnp.concatenate(values_t, axis=0), p.astype(BF))
        att_t[w, :, MAIN : 2 * MAIN] = (out * heads.head_late).astype(BF)

    first_rows = jnp.where(links.lat == 0, AREA // 2, 0)
    lane = iota((AREA, 3 * MAIN), 1)
    query = jnp.where(lane < 2 * MAIN, lane & (MAIN - 1), MAIN)
    seen_apart = (iota((AREA, 3 * MAIN), 0) < first_rows) != (query < first_rows)
    apart[0] = jnp.where(seen_apart, -1e30, 0.0)
    apart[1] = jnp.zeros((AREA, 3 * MAIN), F32)

    def att_to(which):
        return to_targets(spread_q_m, lambda m, w: nt(m, att_t[w]), which)

    gather_window(source, 3, own_n, margin_n)
    fetches[0].wait()
    fetches[1].wait()
    place((3,))
    project(3, 4)
    wait(state_copies)
    normalize(margin, gain[...], margin_n)
    for w in range(3):
        gather_window(source, w, own_n, margin_n)
    place(range(3))
    project(0, 3)
    fetches[2].wait()
    links.arrived(idx_mid, 0, lons)
    links.along_lat(idx_mid, idx_recv, 3, 1)
    att_copies = links.pieces(3, att_send, att_recv, -1)

    def forward_step(w, carry):
        @pl.when(w == 3)
        def _():
            for which in (2, 3, 4):
                first, count_rows, _ = TARGETS[which]
                att_send[pl.ds(first - REACH, count_rows), :] = att_to(which).astype(BF)
            start(att_copies)

        forward(w)
        return carry

    lax.fori_loop(0, 4, forward_step, 0)
    for which in (0, 1):
        first, count_rows, _ = TARGETS[which]
        attended[pl.ds(first, count_rows), :] = att_to(which)

    links.arrived(idx_recv, 3, lats)
    on_lane = iota((n, cap, 128), 2) == iota((n, cap, 128), 1)
    spots = jnp.where(on_lane, idx_recv[...].reshape(n, 1, 128), 0.0)
    spots = jnp.sum(spots, axis=2, keepdims=True).reshape(slots, 1)
    pick = (iota((8, 128), 1) == 0).astype(F32)
    spots_row = lax.dot_general(
        pick,
        jnp.broadcast_to(spots, (slots, 128)),
        (((1,), (1,)), ((), ())),
        precision=lax.Precision.HIGHEST,
        preferred_element_type=F32,
    )[0:1].astype(jnp.int32)
    spots = spots.astype(jnp.int32)
    for first in range(0, slots, 32):
        block = iota((32, CELLS), 1) == spots[first : first + 32]
        onehot[pl.ds(first, 32), :] = block.astype(F32).astype(BF)
    for first in range(0, CELLS, 16):
        block = iota((16, slots), 0) + first == spots_row
        back[pl.ds(first, 16), :] = block.astype(F32).astype(BF)
    back_packed[...] = nn(pack_m[...], back[...]).astype(BF)
    chunk = slots // 2
    per_scale = 1.0 / scale[...]
    wait(fetches[3:7])
    wait(att_copies)
    returned = att_recv[...].astype(F32)
    for first, count_rows, at in RETURNED:
        attended[pl.ds(first, count_rows), :] = returned[at : at + count_rows]
    block_out[...] = (
        state[...].astype(F32) + nn(attended[...].astype(BF), w_out[...])
    ).astype(BF)

    step = min(chunk, 64)
    quarters = [slice(256 * i, 256 * (i + 1)) for i in range(obs_in.shape[1] // 256)]

    def predict(c, carry):
        base = pl.multiple_of(c * chunk, chunk)
        here = pl.ds(base, chunk)
        features = nn(onehot[here, :], block_out[...]).astype(BF)
        for cols in quarters:
            whole = nn(features, obs_in[:, cols])
            for first in range(0, chunk, step):
                pre = whole[first : first + step]
                sig = 0.5 + 0.5 * jnp.tanh(0.5 * pre)
                out = pre * sig
                some = pl.ds(base + first, step)
                hidden[some, cols] = out.astype(BF)
                silu_grad[some, cols] = sig + out * (1.0 - sig)
        predicted[here, :] = nn(hidden[here, :], obs_out[...])
        return carry

    def observe(c, carry):
        base = pl.multiple_of(c * chunk, chunk)
        here = pl.ds(base, chunk)
        lanes = iota((step // cap, cap, 128), 2) == iota((step // cap, cap, 128), 1)
        costs = []
        for first in range(0, chunk, step):
            seen = obs_recv[pl.ds(c * (n // 2) + first // cap, step // cap)].astype(F32)
            seen = jnp.concatenate(
                [seen[:, :cap].reshape(step, half), seen[:, cap:].reshape(step, half)], axis=1
            )
            some = pl.ds(base + first, step)
            residual = (predicted[some, :] - seen) * per_scale
            residuals[some, :] = (residual * per_scale).astype(BF)
            cost = 0.5 * jnp.sum(residual * residual, axis=1, keepdims=True)
            cost = jnp.where(lanes, cost.reshape(step // cap, cap, 1), 0.0)
            costs.append(jnp.sum(cost, axis=1, keepdims=True))
        blocks = pl.ds(c * (lats // 2), lats // 2)
        mis_send[blocks] = jnp.concatenate(costs, axis=0).reshape(lats // 2, lons, 1, 128)
        for cols in quarters:
            whole = nt(residuals[here, :], obs_out[cols, :])
            for first in range(0, chunk, step):
                some = pl.ds(base + first, step)
                grad = whole[first : first + step] * silu_grad[some, cols]
                hidden[some, cols] = grad.astype(BF)
        foot_grad[here, :] = nt(hidden[here, :], obs_in[...]).astype(BF)
        return carry

    lax.fori_loop(0, 2, predict, 0)
    links.arrived(obs_recv, 1, n)
    lax.fori_loop(0, 2, observe, 0)

    to_send = nn(back_packed[...], foot_grad[...]).astype(BF)
    packed_g[...] = nt(to_send, w_out[...]).astype(BF)
    grad_copies = links.pieces(6, packed_g, margin_g, 1)
    start(grad_copies)
    links.along_lon(mis_send, mis_mid, 2, -1)
    state_grad[...] = nn(back[...], foot_grad[...])
    att_grad[...] = nt(state_grad[pl.ds(0, REACH), :].astype(BF), w_out[...]).astype(BF)

    def scores_gradient(p, dp):
        inner = jnp.sum(p * dp, axis=0, keepdims=True)
        return (p * (dp - inner)).astype(BF)

    def backward(w):
        late_q = heads.late_rows(qkv[w, MAIN:AREA, 0:chans])
        late_up = heads.late_rows(win[w, MAIN:AREA, :])
        ups = [heads.stacked(pair_of(win, w, 0, MAIN, pair)) for pair in range(HEADS // 2)]

        def dp_of(pair):
            if pair == HEADS // 2:
                return None
            return nt(pair_of(qkv, w, 2 * chans, AREA, pair), ups[pair])

        after = dp_of(0)
        dp = nt(qkv[w, :, 2 * chans : 3 * chans], late_up)
        keys_t = heads.turned(qkv, w, chans)
        p = probs[w, :, MAIN * HEADS :]
        ds = scores_gradient(p, dp)
        late_dk = nn(ds, late_q)
        late_dv = nn(p.astype(BF), late_up)
        out = nn(jnp.concatenate(keys_t, axis=0), ds)
        dq_t[w, :, MAIN : 2 * MAIN] = (out * (heads.head_late * 0.125)).astype(BF)
        for pair in range(HEADS // 2):
            at = 128 * pair
            dp, after = after, dp_of(pair + 1)
            ds, rounded = [], []
            for h in range(2):
                p = probs[w, :, at * 2 + MAIN * h : at * 2 + MAIN * (h + 1)]
                ds.append(scores_gradient(p, dp[:, MAIN * h : MAIN * (h + 1)]))
                rounded.append(p.astype(BF))
                out = nn(keys_t[pair][64 * h : 64 * h + 64], ds[h])
                dq_t[w, at + 64 * h : at + 64 * h + 64, 0:MAIN] = (out * 0.125).astype(BF)
            dk = nn(
                jnp.concatenate(ds, axis=1), heads.stacked(pair_of(qkv, w, 0, MAIN, pair))
            )
            dv = nn(jnp.concatenate(rounded, axis=1), ups[pair])
            dk_w[w, :, at : at + 128] = (dk + late_dk[:, at : at + 128]).astype(BF)
            dv_w[w, :, at : at + 128] = (dv + late_dv[:, at : at + 128]).astype(BF)

    gather_window(source, 3, att_grad, margin_g)
    place((3,))

    def backward_step(step, carry):
        @pl.when(step == 1)
        def _():
            wait(grad_copies)
            for w in range(3):
                gather_window(source, w, att_grad, margin_g)
            place(range(3))

        @pl.when(step == 2)
        def _():
            links.arrived(mis_mid, 2, lons)
            links.along_lat(mis_mid, mis_recv, 4, -1)

        backward(lax.rem(step + 3, 4))
        return carry

    lax.fori_loop(0, 4, backward_step, 0)

    def project_back(targets):
        for which in targets:
            first, count_rows, _ = TARGETS[which]
            here = pl.ds(first, count_rows)
            proj_grad[here, 0:chans] = to_targets(
                spread_q_m, lambda m, w: nt(m, dq_t[w]), which
            ).astype(BF)
            proj_grad[here, chans : 2 * chans] = to_targets(
                spread_m, lambda m, w: nn(m, dk_w[w]), which
            ).astype(BF)
            proj_grad[here, 2 * chans : 3 * chans] = to_targets(
                spread_m, lambda m, w: nn(m, dv_w[w]), which
            ).astype(BF)

    def norm_part(first, rows, cells, into, more=None):
        whole = nt(proj_grad[pl.ds(first, rows), :], w_in[...])
        step = 48 if rows % 48 == 0 else 16
        for row in range(0, rows, step):
            here = pl.ds(row, step)
            g = gain[...] * whole[row : row + step]
            x = cells[here, :].astype(F32)
            rms = lax.rsqrt(jnp.mean(x * x, axis=-1, keepdims=True) + NORM_EPS)
            inner = jnp.mean(x * g, axis=-1, keepdims=True)
            out = rms * g - x * (rms * rms * rms * inner)
            into[here, :] = out.astype(BF) if more is None else more[here, :] + out

    project_back((2, 3, 4))
    norm_part(REACH, MARGIN, margin, part_send)
    part_copies = links.pieces(9, part_send, part_recv, -1)
    start(part_copies)
    project_back((0, 1))
    norm_part(0, REACH, state, own_part, state_grad)
    own_part[pl.ds(REACH, STRIP), :] = state_grad[pl.ds(REACH, STRIP), :]
    own_store = pltpu.make_async_copy(own_part, own_part_hbm, store_sem.at[0])
    own_store.start()

    links.arrived(mis_recv, 4, lats)
    costs = lax.dot_general(
        mis_recv[...].reshape(n, 128),
        named,
        (((0,), (0,)), ((), ())),
        precision=lax.Precision.HIGHEST,
        preferred_element_type=F32,
    )
    costs = jnp.where(iota((128, feet), 0) == rank, costs, 0.0)
    misfit[...] = jnp.where(live, jnp.sum(costs, axis=0, keepdims=True), 0.0)
    wait(part_copies)
    back_store = pltpu.make_async_copy(part_recv, back_part_hbm, store_sem.at[1])
    back_store.start()
    own_store.wait()
    back_store.wait()


def finish(own_part, back_part, costs, gradient, misfit):
    gradient[...] = own_part[...]
    returned = back_part[...].astype(F32)
    for first, count_rows, at in RETURNED:
        gradient[pl.ds(first, count_rows), :] += returned[at : at + count_rows]
    misfit[...] = costs[...]


def shards(
    lats,
    lons,
    initial_state,
    norm_gain,
    input_weight,
    output_weight,
    obs_in_weight,
    obs_out_weight,
    observed,
    error_scale,
    foot_tile,
    foot_cell,
    foot_count,
):
    n = lats * lons
    chans = initial_state.shape[-1]
    feet, seen = observed.shape
    cap = 2 * feet // n
    slots = n * cap
    pack, gather, spread, spread_q = (jnp.asarray(m, BF) for m in selectors())
    vmem, whole = pl.BlockSpec(memory_space=pltpu.VMEM), pl.BlockSpec(memory_space=pl.ANY)
    state = initial_state.reshape(CELLS, chans)
    gain = norm_gain.reshape(1, chans)
    tile_id = foot_tile.reshape(1, feet)
    count = foot_count.reshape(1, 1)
    limit = 60 * 1024 * 1024

    def shape(*dims, dtype=BF):
        return jax.ShapeDtypeStruct(dims, dtype)

    def room(*dims, dtype=BF):
        return pltpu.VMEM(dims, dtype)

    own_part, back_part, costs = pl.pallas_call(
        functools.partial(kernel, lats, lons, cap),
        out_shape=(
            shape(CELLS, chans, dtype=F32),
            shape(MARGIN, chans),
            shape(1, feet, dtype=F32),
        ),
        in_specs=[whole, vmem] + [whole] * 5 + [vmem] * 4 + [whole] * 4,
        out_specs=(whole, whole, vmem),
        scratch_shapes=[
            room(CELLS, chans),
            room(feet, seen),
            room(MARGIN, CELLS),
            room(*input_weight.shape),
            room(*output_weight.shape),
            room(*obs_in_weight.shape),
            room(*obs_out_weight.shape),
            room(*gather.shape),
            room(*spread.shape),
            room(*spread_q.shape),
            room(MARGIN, chans),
            room(MARGIN, chans),
            room(CELLS, chans),
            room(MARGIN, chans),
            room(4, SRC, chans),
            room(4, AREA, chans),
            room(4, AREA, 3 * chans),
            room(2, AREA, 3 * MAIN, dtype=F32),
            room(4, AREA, MAIN * (HEADS + 1), dtype=F32),
            room(4, chans, 2 * MAIN),
            room(MARGIN, chans),
            room(MARGIN, chans),
            room(CELLS, chans, dtype=F32),
            room(CELLS, chans),
            room(n, 2 * cap, seen // 2),
            room(n, 2 * cap, seen // 2),
            room(lats, lons, 1, 128, dtype=F32),
            room(lons, lats, 1, 128, dtype=F32),
            room(lats, lons, 1, 128, dtype=F32),
            room(lats, lons, 1, 128, dtype=F32),
            room(lons, lats, 1, 128, dtype=F32),
            room(lats, lons, 1, 128, dtype=F32),
            room(slots, feet),
            room(slots, obs_in_weight.shape[1], dtype=F32),
            room(slots, obs_in_weight.shape[1]),
            room(slots, seen, dtype=F32),
            room(slots, seen),
            room(slots, chans),
            room(slots, CELLS),
            room(CELLS, slots),
            room(MARGIN, slots),
            room(CELLS, chans, dtype=F32),
            room(REACH, chans),
            room(MARGIN, chans),
            room(MARGIN, chans),
            room(4, AREA, chans),
            room(4, AREA, chans),
            room(4, chans, 2 * MAIN),
            room(REACH + MARGIN, 3 * chans),
            room(MARGIN, chans),
            room(MARGIN, chans),
            room(CELLS, chans, dtype=F32),
            pltpu.SemaphoreType.DMA((24,)),
            pltpu.SemaphoreType.DMA((10,)),
            pltpu.SemaphoreType.DMA((10,)),
            pltpu.SemaphoreType.DMA((2,)),
            pltpu.SemaphoreType.REGULAR,
        ],
        compiler_params=pltpu.CompilerParams(
            collective_id=0, has_side_effects=True, vmem_limit_bytes=limit
        ),
    )(
        state,
        gain,
        input_weight,
        output_weight,
        obs_in_weight,
        obs_out_weight,
        observed,
        error_scale.reshape(1, seen),
        tile_id,
        foot_cell.reshape(1, feet),
        count,
        pack,
        gather,
        spread,
        spread_q,
    )
    gradient, misfit = pl.pallas_call(
        finish,
        out_shape=(shape(CELLS, chans, dtype=F32), shape(1, feet, dtype=F32)),
        in_specs=[vmem] * 3,
        out_specs=(vmem, vmem),
    )(own_part, back_part, costs)
    return gradient.reshape(initial_state.shape), misfit.reshape(feet)


def solution(mesh):
    both = ("lat", "lon")
    placed = (
        P("lat", "lon", None),
        P(),
        P(),
        P(),
        P(),
        P(),
        P(both, None),
        P(),
        P(both, None),
        P(both),
        P(both),
    )
    return jax.shard_map(
        functools.partial(shards, mesh.shape["lat"], mesh.shape["lon"]),
        mesh=mesh,
        in_specs=placed,
        out_specs=(P("lat", "lon", None), P(both)),
        check_vma=False,
    )
```

time: 369 us -> 64.2 us (0.17)
  local copies, waits for them, and re-layouts: 120 us -> 0 us
  matrix products: 114 us -> 0 us
  waiting for transfers between devices: 64.8 us -> 0 us
  Pallas kernels: 0 us -> 62.7 us
  starting transfers between devices: 38.4 us -> 0 us
  other arithmetic: 27.5 us -> 0 us
    dot_general x22 -> x0, matrix products: 86 us -> none  [the longest x3 22.7 us: band_backward(): jnp.einsum('nhqk,nkhe->nqhe', score_grad, keys, preferred_element_type=jn...]
    pallas_call x0 -> x2, Pallas kernels: none -> 62.7 us  [the longest x1 60.2 us: shards(): pl.pallas_call(functools.partial(kernel, lats, lons, cap), out_shape=(sha...]
    all_to_all x3 -> x0, waiting for transfers between devices: 40.7 us -> none  [the longest x1 16.6 us: shards(): lax.all_to_all(grad_buf, ('lat', 'lon'), split_axis=0, concat_axis=0, til...]
    sub x6 -> x0, matrix products: 27.7 us -> none  [softmax_weights(): expo = jnp.exp(scores - top)]
    ppermute x8 -> x0, waiting for transfers between devices: 24.1 us -> none  [the longest x4 14.2 us: extended_2(): after = lax.ppermute(first, axis, down)]
    all_to_all x3 -> x0, starting transfers between devices: 22.9 us -> none  [the longest x1 9.51 us: shards(): lax.all_to_all(request_buf, ('lat', 'lon'), split_axis=0, concat_axis=0,...]
    reshape x5 -> x0, local copies, waits for them, and re-layouts: 21.6 us -> none  [the longest x2 11.1 us: from_window_order(): return shaped.reshape(bands * WIN, nwin * WIN, chans)]
    ppermute x8 -> x0, starting transfers between devices: 15.4 us -> none  [the longest x4 10.3 us: extended_2(): before = lax.ppermute(last, axis, up)]
  transfers between devices with their start and end apart: 11 -> 0, of which waited for: 9 -> 0; matrix products, arithmetic and copies ran while one was open for 2% -> 0% of each run, Pallas kernels for 0% -> 0%
where the time goes in v1:
time: 64.2 us; the launch traced here: 64 us
  Pallas kernels  62.7 us (98%)
  between operations  1.29 us (2%)
    pallas_call x1, Pallas kernels, shards(): pl.pallas_call(functools.partial(kernel, lats, lons, cap), out_shape=(sha...  60.2 us
    pallas_call x1, Pallas kernels, shards(): pl.pallas_call(finish, out_shape=(shape(CELLS, chans, dtype=F32), shape(1...  2.56 us

profile of v1, /device:TPU:25, one launch (start us, length us, event | category | flops | bytes accessed | tf_op | source)
XLA Modules:
  0.0 64.0 jit_solution(16568216785652491516)
XLA Ops:
  1.3 60.2 %shard_map.158 = (f32[576,512]{1,0:T(8,128)}, bf16[272,512]{1,0:T(8,128)(2,1)}, f32[1,512]{1,0:T(1,128)}) custom-call(bf16[576,512]{1,0:T(8,128)(2,1)} %bitcast.9, f32[1,512]{1,0:T(1,128)} %bitcast.10, bf16[512,1536]{1,0:T(8,128)(2,1)} %w_in_hbm.1, bf16[512,512]{1,0:T(8,128)(2,1)} %w_out_hbm.1, bf16[512,1024]{1,0:T(8,128)(2,1)} %obs_in_hbm.1, ...), custom_call_target="tpu_custom_call" | custom-call | tf_op jit(solution)/shard_map/pallas_call | solution.py:744
  61.5 2.6 %shard_map.159 = (f32[576,512]{1,0:T(8,128)}, f32[1,512]{1,0:T(1,128)}) custom-call(f32[576,512]{1,0:T(8,128)} %get-tuple-element.7.own_part, bf16[272,512]{1,0:T(8,128)(2,1)} %get-tuple-element.8.back_part, f32[1,512]{1,0:T(1,128)} %get-tuple-element.9.costs), custom_call_target="tpu_custom_call" | custom-call | tf_op jit(solution)/shard_map/pallas_call | solution.py:832

commit v2 on v1

--- a/solution.py
+++ b/solution.py
@@ -23,7 +23,7 @@
 BF = jnp.bfloat16
 F32 = jnp.float32
 
-WINDOWS = ((1, 0), (0, 1), (0, 0), (1, 1))
+WINDOWS = ((0, 0), (0, 1), (1, 0), (1, 1))
 REACH = 3 * STRIP
 ACROSS = SIDE - HALF
 SIDES, CORNER = 112, 48
@@ -31,17 +31,17 @@
 MARGIN = 2 * SIDES + CORNER
 PIECES = ((LEFT, SIDES, 0, 1), (TOP, SIDES, 1, 0), (TL, CORNER, 1, 1))
 SOURCES = (
+    ((True, 0, 176), (False, TOP, SIDES), (False, LEFT, 48), (False, TL, CORNER)),
+    ((True, 0, 272), (False, TOP, SIDES)),
     ((True, 144, 288), (False, LEFT + 32, 80), (True, 0, 16)),
-    ((True, 0, 272), (False, TOP, SIDES)),
-    ((True, 0, 176), (False, TOP, SIDES), (False, LEFT, 48), (False, TL, CORNER)),
     ((True, 144, 288), (True, 0, 96)),
 )
 TARGETS = (
-    (0, STRIP, (1, 2)),
-    (STRIP, 2 * STRIP, (0, 3)),
+    (0, STRIP, (0, 1)),
+    (STRIP, 2 * STRIP, (2, 3)),
     (REACH + LEFT, SIDES, (0, 2)),
-    (REACH + TOP, SIDES, (1, 2)),
-    (REACH + TL, CORNER, (2,)),
+    (REACH + TOP, SIDES, (0, 1)),
+    (REACH + TL, CORNER, (0,)),
 )
 
 
@@ -125,10 +125,10 @@
 
 
 class Links:
-    def __init__(self, lats, lons, margin_sem, foot_sem, line_sem):
+    def __init__(self, lats, lons, margin_sem, foot_sem):
         self.lats, self.lons, self.n = lats, lons, lats * lons
         self.lat, self.lon = lax.axis_index("lat"), lax.axis_index("lon")
-        self.margin_sem, self.foot_sem, self.line_sem = margin_sem, foot_sem, line_sem
+        self.margin_sem, self.foot_sem = margin_sem, foot_sem
         self.barrier = pltpu.get_barrier_semaphore()
 
     def around(self, up, right):
@@ -136,22 +136,16 @@
         return lax.rem(self.lat + up + lats, lats), lax.rem(self.lon + right + lons, lons)
 
     def away_by(self, d):
-        return self.around(d // self.lons, d % self.lons)
-
-    def signal(self, sem, device):
-        pl.semaphore_signal(sem, inc=1, device_id=device, device_id_type=MESH)
-
-    def greet(self):
-        for step in range(1, self.lats):
-            self.signal(self.barrier, self.around(step, 0))
-        for step in range(1, self.lons):
-            self.signal(self.barrier, self.around(0, step))
-
-    def met(self):
-        pl.semaphore_wait(self.barrier, self.lats - 1 + self.lons - 1)
-        for step in range(1, self.lats):
-            self.signal(self.line_sem, self.around(step, 0))
-        pl.semaphore_wait(self.line_sem, self.lats - 1)
+        return self.around(lax.rem(d, self.lats), d // self.lats)
+
+    def greet(self, device):
+        pl.semaphore_signal(self.barrier, inc=1, device_id=device, device_id_type=MESH)
+
+    def greet_all(self):
+        each(1, self.n, lambda d: self.greet(self.away_by(d)))
+
+    def met_all(self):
+        pl.semaphore_wait(self.barrier, self.n - 1)
 
     def copy(self, sems, i, src, dst, device):
         return pltpu.make_async_remote_copy(
@@ -180,32 +174,32 @@
         self.copy(self.foot_sem, i, rest, rest, self.around(1, 0)).wait()
 
     def to_all(self, send, into, i):
-        def one(d):
-            self.copy(self.foot_sem, i, send.at[d], into.at[d], self.away_by(d)).start()
-
-        steps = (self.n - 1) // 7
-
-        def seven(k, carry):
-            for j in range(7):
-                one(1 + 7 * k + j)
-            return carry
-
-        lax.fori_loop(0, steps, seven, 0)
-        for d in range(1 + 7 * steps, self.n):
-            one(d)
+        each(
+            1,
+            self.n,
+            lambda d: self.copy(self.foot_sem, i, send.at[d], into.at[d], self.away_by(d)).start(),
+        )
         into[0] = send[0]
 
-    def along_lon(self, send, into, i, way):
-        for step in range(1, self.lons):
-            device = self.around(0, way * step)
-            self.copy(self.foot_sem, i, send.at[:, step], into.at[step], device).start()
+    def back_lat(self, send, into, i):
+        each(
+            1,
+            self.lats,
+            lambda step: self.copy(
+                self.foot_sem, i, send.at[:, step], into.at[step], self.around(-step, 0)
+            ).start(),
+        )
         into[0] = send[:, 0]
 
-    def along_lat(self, send, into, i, way):
-        for step in range(1, self.lats):
-            device = self.around(way * step, 0)
-            self.copy(self.foot_sem, i, send.at[:, step], into.at[step], device).start()
-        into[0] = send[:, 0]
+    def back_lon(self, mid, into, i):
+        each(
+            1,
+            self.lons,
+            lambda step: self.copy(
+                self.foot_sem, i, mid.at[:, step], into.at[step], self.around(0, -step)
+            ).start(),
+        )
+        into[0] = mid[:, 0]
 
 
 def footprint_places(links, tile_id, count, cap):
@@ -214,7 +208,7 @@
     tile_lat = jnp.floor((tile_id[...].astype(F32) + 0.5) * (1.0 / lons)).astype(jnp.int32)
     up, right = tile_lat - links.lat, tile_id[...] - tile_lat * lons - links.lon
     up, right = jnp.where(up < 0, up + lats, up), jnp.where(right < 0, right + lons, right)
-    away = up * lons + right
+    away = right * lats + up
     live = iota((1, feet), 1) < count[...]
     named = (iota((n, feet), 0) == away).astype(F32)
     before = (iota((feet, feet), 0) < iota((feet, feet), 1)).astype(F32).astype(BF)
@@ -322,7 +316,6 @@
     obs_send,
     obs_recv,
     idx_send,
-    idx_mid,
     idx_recv,
     mis_send,
     mis_mid,
@@ -351,10 +344,8 @@
     foot_sem,
     fetch_sem,
     store_sem,
-    line_sem,
 ):
-    links = Links(lats, lons, margin_sem, foot_sem, line_sem)
-    links.greet()
+    links = Links(lats, lons, margin_sem, foot_sem)
     n = links.n
     slots = n * cap
     feet = tile_id.shape[1]
@@ -377,13 +368,13 @@
         )
     ]
     start(fetches[7:])
+    links.greet_all()
     start(fetches[:7])
-    fetches[7].wait()
-    fetches[8].wait()
+    wait(fetches[7:9])
 
     packed[...] = nn(pack_m[...], state[...]).astype(BF)
 
-    links.met()
+    links.met_all()
     state_copies = links.pieces(0, packed, margin, 1)
     start(state_copies)
 
@@ -398,14 +389,14 @@
         cell = jnp.sum(block * cell_value, axis=1, keepdims=True) - 1.0
         cell = jnp.where(on_lane, cell.reshape(4, cap, 1), 0.0)
         cells.append(jnp.sum(cell, axis=1, keepdims=True))
-    idx_send[...] = jnp.concatenate(cells, axis=0).reshape(lats, lons, 1, 128)
-    links.along_lon(idx_send, idx_mid, 0, 1)
+    idx_send[...] = jnp.concatenate(cells, axis=0)
     fetches[9].wait()
     rows = nn(chosen[...], observed[...])
     half = rows.shape[1] // 2
     rows = rows.reshape(n, cap, 2 * half)
     obs_send[...] = jnp.concatenate([rows[:, :, :half], rows[:, :, half:]], axis=1).astype(BF)
 
+    links.to_all(idx_send, idx_recv, 0)
     links.to_all(obs_send, obs_recv, 1)
 
     normalize(state, gain[...], own_n)
@@ -429,7 +420,7 @@
         return e * (1.0 / jnp.sum(e, axis=0, keepdims=True))
 
     def forward(w):
-        row = jnp.where((w == 1) | (w == 2), 0, 1)
+        row = jnp.where(w < 2, 0, 1)
         late = heads.late_rows(qkv[w, MAIN:AREA, 0:chans])
         values_t = heads.turned(qkv, w, 2 * chans)
 
@@ -476,17 +467,17 @@
     place(range(3))
     project(0, 3)
     fetches[2].wait()
-    links.arrived(idx_mid, 0, lons)
-    links.along_lat(idx_mid, idx_recv, 3, 1)
     att_copies = links.pieces(3, att_send, att_recv, -1)
 
     def forward_step(w, carry):
-        @pl.when(w == 3)
-        def _():
-            for which in (2, 3, 4):
-                first, count_rows, _ = TARGETS[which]
-                att_send[pl.ds(first - REACH, count_rows), :] = att_to(which).astype(BF)
-            start(att_copies)
+        for at, targets, some in ((2, (3, 4), att_copies[1:]), (3, (2,), att_copies[:1])):
+
+            @pl.when(w == at)
+            def _():
+                for which in targets:
+                    first, count_rows, _ = TARGETS[which]
+                    att_send[pl.ds(first - REACH, count_rows), :] = att_to(which).astype(BF)
+                start(some)
 
         forward(w)
         return carry
@@ -496,9 +487,9 @@
         first, count_rows, _ = TARGETS[which]
         attended[pl.ds(first, count_rows), :] = att_to(which)
 
-    links.arrived(idx_recv, 3, lats)
+    links.arrived(idx_recv, 0, n)
     on_lane = iota((n, cap, 128), 2) == iota((n, cap, 128), 1)
-    spots = jnp.where(on_lane, idx_recv[...].reshape(n, 1, 128), 0.0)
+    spots = jnp.where(on_lane, idx_recv[...], 0.0)
     spots = jnp.sum(spots, axis=2, keepdims=True).reshape(slots, 1)
     pick = (iota((8, 128), 1) == 0).astype(F32)
     spots_row = lax.dot_general(
@@ -562,8 +553,8 @@
             cost = 0.5 * jnp.sum(residual * residual, axis=1, keepdims=True)
             cost = jnp.where(lanes, cost.reshape(step // cap, cap, 1), 0.0)
             costs.append(jnp.sum(cost, axis=1, keepdims=True))
-        blocks = pl.ds(c * (lats // 2), lats // 2)
-        mis_send[blocks] = jnp.concatenate(costs, axis=0).reshape(lats // 2, lons, 1, 128)
+        blocks = pl.ds(c * (lons // 2), lons // 2)
+        mis_send[blocks] = jnp.concatenate(costs, axis=0).reshape(lons // 2, lats, 1, 128)
         for cols in quarters:
             whole = nt(residuals[here, :], obs_out[cols, :])
             for first in range(0, chunk, step):
@@ -581,7 +572,7 @@
     packed_g[...] = nt(to_send, w_out[...]).astype(BF)
     grad_copies = links.pieces(6, packed_g, margin_g, 1)
     start(grad_copies)
-    links.along_lon(mis_send, mis_mid, 2, -1)
+    links.back_lat(mis_send, mis_mid, 2)
     state_grad[...] = nn(back[...], foot_grad[...])
     att_grad[...] = nt(state_grad[pl.ds(0, REACH), :].astype(BF), w_out[...]).astype(BF)
 
@@ -625,27 +616,6 @@
             dk_w[w, :, at : at + 128] = (dk + late_dk[:, at : at + 128]).astype(BF)
             dv_w[w, :, at : at + 128] = (dv + late_dv[:, at : at + 128]).astype(BF)
 
-    gather_window(source, 3, att_grad, margin_g)
-    place((3,))
-
-    def backward_step(step, carry):
-        @pl.when(step == 1)
-        def _():
-            wait(grad_copies)
-            for w in range(3):
-                gather_window(source, w, att_grad, margin_g)
-            place(range(3))
-
-        @pl.when(step == 2)
-        def _():
-            links.arrived(mis_mid, 2, lons)
-            links.along_lat(mis_mid, mis_recv, 4, -1)
-
-        backward(lax.rem(step + 3, 4))
-        return carry
-
-    lax.fori_loop(0, 4, backward_step, 0)
-
     def project_back(targets):
         for which in targets:
             first, count_rows, _ = TARGETS[which]
@@ -660,11 +630,11 @@
                 spread_m, lambda m, w: nn(m, dv_w[w]), which
             ).astype(BF)
 
-    def norm_part(first, rows, cells, into, more=None):
+    def norm_part(first, rows, cells, at, into, more=None):
         whole = nt(proj_grad[pl.ds(first, rows), :], w_in[...])
         step = 48 if rows % 48 == 0 else 16
         for row in range(0, rows, step):
-            here = pl.ds(row, step)
+            here = pl.ds(at + row, step)
             g = gain[...] * whole[row : row + step]
             x = cells[here, :].astype(F32)
             rms = lax.rsqrt(jnp.mean(x * x, axis=-1, keepdims=True) + NORM_EPS)
@@ -672,17 +642,44 @@
             out = rms * g - x * (rms * rms * rms * inner)
             into[here, :] = out.astype(BF) if more is None else more[here, :] + out
 
-    project_back((2, 3, 4))
-    norm_part(REACH, MARGIN, margin, part_send)
     part_copies = links.pieces(9, part_send, part_recv, -1)
-    start(part_copies)
+    gather_window(source, 3, att_grad, margin_g)
+    place((3,))
+
+    def backward_step(step, carry):
+        @pl.when(step == 1)
+        def _():
+            wait(grad_copies)
+            for w in range(3):
+                gather_window(source, w, att_grad, margin_g)
+            place(range(3))
+
+        @pl.when(step == 2)
+        def _():
+            links.arrived(mis_mid, 2, lats)
+            links.back_lon(mis_mid, mis_recv, 3)
+
+        @pl.when(step == 3)
+        def _():
+            project_back((3, 4))
+            norm_part(REACH + TOP, MARGIN - TOP, margin, TOP, part_send)
+            start(part_copies[1:])
+
+        backward(lax.rem(step + 3, 4))
+        return carry
+
+    lax.fori_loop(0, 4, backward_step, 0)
+
+    project_back((2,))
+    norm_part(REACH + LEFT, SIDES, margin, LEFT, part_send)
+    start(part_copies[:1])
     project_back((0, 1))
-    norm_part(0, REACH, state, own_part, state_grad)
+    norm_part(0, REACH, state, 0, own_part, state_grad)
     own_part[pl.ds(REACH, STRIP), :] = state_grad[pl.ds(REACH, STRIP), :]
     own_store = pltpu.make_async_copy(own_part, own_part_hbm, store_sem.at[0])
     own_store.start()
 
-    links.arrived(mis_recv, 4, lats)
+    links.arrived(mis_recv, 3, lons)
     costs = lax.dot_general(
         mis_recv[...].reshape(n, 128),
         named,
@@ -777,12 +774,11 @@
             room(CELLS, chans),
             room(n, 2 * cap, seen // 2),
             room(n, 2 * cap, seen // 2),
+            room(n, 1, 128, dtype=F32),
+            room(n, 1, 128, dtype=F32),
+            room(lons, lats, 1, 128, dtype=F32),
             room(lats, lons, 1, 128, dtype=F32),
             room(lons, lats, 1, 128, dtype=F32),
-            room(lats, lons, 1, 128, dtype=F32),
-            room(lats, lons, 1, 128, dtype=F32),
-            room(lons, lats, 1, 128, dtype=F32),
-            room(lats, lons, 1, 128, dtype=F32),
             room(slots, feet),
             room(slots, obs_in_weight.shape[1], dtype=F32),
             room(slots, obs_in_weight.shape[1]),
@@ -804,10 +800,9 @@
             room(MARGIN, chans),
             room(CELLS, chans, dtype=F32),
             pltpu.SemaphoreType.DMA((24,)),
-            pltpu.SemaphoreType.DMA((10,)),
+            pltpu.SemaphoreType.DMA((8,)),
             pltpu.SemaphoreType.DMA((10,)),
             pltpu.SemaphoreType.DMA((2,)),
-            pltpu.SemaphoreType.REGULAR,
         ],
         compiler_params=pltpu.CompilerParams(
             collective_id=0, has_side_effects=True, vmem_limit_bytes=limit

time: 64.2 us -> 61.5 us (0.958)
  Pallas kernels: 62.7 us -> 60 us
    pallas_call x1, Pallas kernels: 60.2 us -> 57.5 us  [shards(): pl.pallas_call(functools.partial(kernel, lats, lons, cap), out_shape=(sha...]
where the time goes in v2:
time: 61.5 us; the launch traced here: 61.3 us
  Pallas kernels  60 us (98%)
  between operations  1.29 us (2%)
    pallas_call x1, Pallas kernels, shards(): pl.pallas_call(functools.partial(kernel, lats, lons, cap), out_shape=(sha...  57.5 us
    pallas_call x1, Pallas kernels, shards(): pl.pallas_call(finish, out_shape=(shape(CELLS, chans, dtype=F32), shape(1...  2.56 us

profile of v2, /device:TPU:25, one launch (start us, length us, event | category | flops | bytes accessed | tf_op | source)
XLA Modules:
  0.0 61.3 jit_solution(2771614535287406753)
XLA Ops:
  1.3 57.5 %shard_map.158 = (f32[576,512]{1,0:T(8,128)}, bf16[272,512]{1,0:T(8,128)(2,1)}, f32[1,512]{1,0:T(1,128)}) custom-call(bf16[576,512]{1,0:T(8,128)(2,1)} %bitcast.9, f32[1,512]{1,0:T(1,128)} %bitcast.10, bf16[512,1536]{1,0:T(8,128)(2,1)} %w_in_hbm.1, bf16[512,512]{1,0:T(8,128)(2,1)} %w_out_hbm.1, bf16[512,1024]{1,0:T(8,128)(2,1)} %obs_in_hbm.1, ...), custom_call_target="tpu_custom_call" | custom-call | tf_op jit(solution)/shard_map/pallas_call | solution.py:741
  58.8 2.6 %shard_map.159 = (f32[576,512]{1,0:T(8,128)}, f32[1,512]{1,0:T(1,128)}) custom-call(f32[576,512]{1,0:T(8,128)} %get-tuple-element.7.own_part, bf16[272,512]{1,0:T(8,128)(2,1)} %get-tuple-element.8.back_part, f32[1,512]{1,0:T(1,128)} %get-tuple-element.9.costs), custom_call_target="tpu_custom_call" | custom-call | tf_op jit(solution)/shard_map/pallas_call | solution.py:827

commit v3 on v2

--- a/solution.py
+++ b/solution.py
@@ -272,26 +272,32 @@
     lons,
     cap,
     state_hbm,
-    gain,
+    gain_hbm,
     w_in_hbm,
     w_out_hbm,
     obs_in_hbm,
     obs_out_hbm,
     observed_hbm,
-    scale,
-    tile_id,
-    cell_id,
-    count,
+    scale_hbm,
+    tile_id_hbm,
+    cell_id_hbm,
+    count_hbm,
     pack_hbm,
     gather_hbm,
     spread_hbm,
     spread_q_hbm,
     own_part_hbm,
     back_part_hbm,
-    misfit,
+    misfit_hbm,
     state,
     observed,
     pack_m,
+    gain,
+    scale,
+    tile_id,
+    cell_id,
+    count,
+    misfit,
     w_in,
     w_out,
     obs_in,
@@ -336,6 +342,7 @@
     dk_w,
     dv_w,
     dq_t,
+    keys_t,
     proj_grad,
     part_send,
     part_recv,
@@ -364,11 +371,17 @@
                 (state_hbm, state),
                 (pack_hbm, pack_m),
                 (observed_hbm, observed),
+                (gain_hbm, gain),
+                (scale_hbm, scale),
+                (tile_id_hbm, tile_id),
+                (cell_id_hbm, cell_id),
+                (count_hbm, count),
             )
         )
     ]
-    start(fetches[7:])
+    start(fetches[7:9])
     links.greet_all()
+    start(fetches[9:])
     start(fetches[:7])
     wait(fetches[7:9])
 
@@ -378,6 +391,7 @@
     state_copies = links.pieces(0, packed, margin, 1)
     start(state_copies)
 
+    wait(fetches[10:])
     away, rank, live, named = footprint_places(links, tile_id, count, cap)
     slot = jnp.where(live, away * cap + rank, -1)
     cell_value = (cell_id[...] + 1).astype(F32)
@@ -576,6 +590,12 @@
     state_grad[...] = nn(back[...], foot_grad[...])
     att_grad[...] = nt(state_grad[pl.ds(0, REACH), :].astype(BF), w_out[...]).astype(BF)
 
+    def turn_keys(w, carry):
+        keys_t[w] = jnp.concatenate(heads.turned(qkv, w, chans), axis=0)
+        return carry
+
+    lax.fori_loop(0, 4, turn_keys, 0)
+
     def scores_gradient(p, dp):
         inner = jnp.sum(p * dp, axis=0, keepdims=True)
         return (p * (dp - inner)).astype(BF)
@@ -592,12 +612,11 @@
 
         after = dp_of(0)
         dp = nt(qkv[w, :, 2 * chans : 3 * chans], late_up)
-        keys_t = heads.turned(qkv, w, chans)
         p = probs[w, :, MAIN * HEADS :]
         ds = scores_gradient(p, dp)
         late_dk = nn(ds, late_q)
         late_dv = nn(p.astype(BF), late_up)
-        out = nn(jnp.concatenate(keys_t, axis=0), ds)
+        out = nn(keys_t[w], ds)
         dq_t[w, :, MAIN : 2 * MAIN] = (out * (heads.head_late * 0.125)).astype(BF)
         for pair in range(HEADS // 2):
             at = 128 * pair
@@ -607,8 +626,8 @@
                 p = probs[w, :, at * 2 + MAIN * h : at * 2 + MAIN * (h + 1)]
                 ds.append(scores_gradient(p, dp[:, MAIN * h : MAIN * (h + 1)]))
                 rounded.append(p.astype(BF))
-                out = nn(keys_t[pair][64 * h : 64 * h + 64], ds[h])
-                dq_t[w, at + 64 * h : at + 64 * h + 64, 0:MAIN] = (out * 0.125).astype(BF)
+                rows = slice(at + 64 * h, at + 64 * h + 64)
+                dq_t[w, rows, 0:MAIN] = (nn(keys_t[w, rows, :], ds[h]) * 0.125).astype(BF)
             dk = nn(
                 jnp.concatenate(ds, axis=1), heads.stacked(pair_of(qkv, w, 0, MAIN, pair))
             )
@@ -689,11 +708,12 @@
     )
     costs = jnp.where(iota((128, feet), 0) == rank, costs, 0.0)
     misfit[...] = jnp.where(live, jnp.sum(costs, axis=0, keepdims=True), 0.0)
+    misfit_store = pltpu.make_async_copy(misfit, misfit_hbm, store_sem.at[2])
+    misfit_store.start()
     wait(part_copies)
     back_store = pltpu.make_async_copy(part_recv, back_part_hbm, store_sem.at[1])
     back_store.start()
-    own_store.wait()
-    back_store.wait()
+    wait([own_store, misfit_store, back_store])
 
 
 def finish(own_part, back_part, costs, gradient, misfit):
@@ -745,12 +765,18 @@
             shape(MARGIN, chans),
             shape(1, feet, dtype=F32),
         ),
-        in_specs=[whole, vmem] + [whole] * 5 + [vmem] * 4 + [whole] * 4,
-        out_specs=(whole, whole, vmem),
+        in_specs=[whole] * 15,
+        out_specs=(whole,) * 3,
         scratch_shapes=[
             room(CELLS, chans),
             room(feet, seen),
             room(MARGIN, CELLS),
+            room(1, chans, dtype=F32),
+            room(1, seen, dtype=F32),
+            room(1, feet, dtype=jnp.int32),
+            room(1, feet, dtype=jnp.int32),
+            room(1, 1, dtype=jnp.int32),
+            room(1, feet, dtype=F32),
             room(*input_weight.shape),
             room(*output_weight.shape),
             room(*obs_in_weight.shape),
@@ -795,14 +821,15 @@
             room(4, AREA, chans),
             room(4, AREA, chans),
             room(4, chans, 2 * MAIN),
+            room(4, chans, AREA),
             room(REACH + MARGIN, 3 * chans),
             room(MARGIN, chans),
             room(MARGIN, chans),
             room(CELLS, chans, dtype=F32),
             pltpu.SemaphoreType.DMA((24,)),
             pltpu.SemaphoreType.DMA((8,)),
-            pltpu.SemaphoreType.DMA((10,)),
-            pltpu.SemaphoreType.DMA((2,)),
+            pltpu.SemaphoreType.DMA((15,)),
+            pltpu.SemaphoreType.DMA((3,)),
         ],
         compiler_params=pltpu.CompilerParams(
             collective_id=0, has_side_effects=True, vmem_limit_bytes=limit

time: 61.5 us -> 60.8 us (0.989)
  Pallas kernels: 60 us -> 59.3 us
    pallas_call x1, Pallas kernels: 57.5 us -> 56.8 us  [shards(): pl.pallas_call(functools.partial(kernel, lats, lons, cap), out_shape=(sha...]
where the time goes in v3:
time: 60.8 us; the launch traced here: 60.6 us
  Pallas kernels  59.3 us (98%)
  between operations  1.29 us (2%)
    pallas_call x1, Pallas kernels, shards(): pl.pallas_call(functools.partial(kernel, lats, lons, cap), out_shape=(sha...  56.8 us
    pallas_call x1, Pallas kernels, shards(): pl.pallas_call(finish, out_shape=(shape(CELLS, chans, dtype=F32), shape(1...  2.56 us

profile of v3, /device:TPU:25, one launch (start us, length us, event | category | flops | bytes accessed | tf_op | source)
XLA Modules:
  0.0 60.6 jit_solution(4086728776323726457)
XLA Ops:
  1.3 56.8 %shard_map.158 = (f32[576,512]{1,0:T(8,128)}, bf16[272,512]{1,0:T(8,128)(2,1)}, f32[1,512]{1,0:T(1,128)}) custom-call(bf16[576,512]{1,0:T(8,128)(2,1)} %bitcast.9, f32[1,512]{1,0:T(1,128)} %bitcast.10, bf16[512,1536]{1,0:T(8,128)(2,1)} %w_in_hbm.1, bf16[512,512]{1,0:T(8,128)(2,1)} %w_out_hbm.1, bf16[512,1024]{1,0:T(8,128)(2,1)} %obs_in_hbm.1, ...), custom_call_target="tpu_custom_call" | custom-call | tf_op jit(solution)/shard_map/pallas_call | solution.py:761
  58.1 2.6 %shard_map.159 = (f32[576,512]{1,0:T(8,128)}, f32[1,512]{1,0:T(1,128)}) custom-call(f32[576,512]{1,0:T(8,128)} %get-tuple-element.7.own_part, bf16[272,512]{1,0:T(8,128)(2,1)} %get-tuple-element.8.back_part, f32[1,512]{1,0:T(1,128)} %get-tuple-element.9.costs), custom_call_target="tpu_custom_call" | custom-call | tf_op jit(solution)/shard_map/pallas_call | solution.py:854

commit v4 on v3

--- a/solution.py
+++ b/solution.py
@@ -220,11 +220,8 @@
     def __init__(self, chans):
         self.even = (iota((1, 128), 1) < 64).astype(F32).astype(BF)
         self.odd = (iota((1, 128), 1) >= 64).astype(F32).astype(BF)
-        self.eye = (iota((128, 128), 0) == iota((128, 128), 1)).astype(F32).astype(BF)
         late_head = iota((MAIN, chans), 0) >> 4 == iota((MAIN, chans), 1) >> 6
         self.late_head = late_head.astype(F32).astype(BF)
-        head_late = iota((chans, MAIN), 0) >> 6 == iota((chans, MAIN), 1) >> 4
-        self.head_late = head_late.astype(F32)
 
     def stacked(self, x):
         return jnp.concatenate([x * self.even, x * self.odd], axis=0)
@@ -233,10 +230,10 @@
         return jnp.concatenate([x] * HEADS, axis=0) * self.late_head
 
     def turned(self, qkv, w, first):
-        return [
-            nt(self.eye, pair_of(qkv, w, first, AREA, pair)).astype(BF)
-            for pair in range(HEADS // 2)
-        ]
+        return [pair_of(qkv, w, first, AREA, pair).T for pair in range(HEADS // 2)]
+
+    def late_out(self, x, held):
+        return nn(x.T, held).astype(BF) * self.late_head
 
 
 def pair_of(ref, w, first, rows, pair):
@@ -314,7 +311,7 @@
     qkv,
     apart,
     probs,
-    att_t,
+    att_w,
     att_send,
     att_recv,
     attended,
@@ -341,7 +338,7 @@
     margin_g,
     dk_w,
     dv_w,
-    dq_t,
+    dq_w,
     keys_t,
     proj_grad,
     part_send,
@@ -447,17 +444,17 @@
         after = scored(0)
         for pair in range(HEADS // 2):
             scores, after = after, scored(pair + 1)
+            out = []
             for h in range(2):
                 lanes = slice(MAIN * h, MAIN * (h + 1))
                 p = softmax(scores[:, lanes] + apart[row, :, lanes])
                 probs[w, :, 256 * pair + MAIN * h : 256 * pair + MAIN * (h + 1)] = p
-                at = 128 * pair + 64 * h
-                out = nn(values_t[pair][64 * h : 64 * h + 64], p.astype(BF))
-                att_t[w, at : at + 64, 0:MAIN] = out.astype(BF)
+                out.append(nn(values_t[pair][64 * h : 64 * h + 64], p.astype(BF)))
+            out = jnp.concatenate(out, axis=0).astype(BF)
+            att_w[w, 0:MAIN, 128 * pair : 128 * (pair + 1)] = out.T
         p = softmax(after + apart[row, :, 2 * MAIN :])
         probs[w, :, MAIN * HEADS :] = p
-        out = nn(jnp.concatenate(values_t, axis=0), p.astype(BF))
-        att_t[w, :, MAIN : 2 * MAIN] = (out * heads.head_late).astype(BF)
+        att_w[w, MAIN : 2 * MAIN, :] = heads.late_out(p.astype(BF), qkv[w, :, 2 * chans :])
 
     first_rows = jnp.where(links.lat == 0, AREA // 2, 0)
     lane = iota((AREA, 3 * MAIN), 1)
@@ -466,8 +463,8 @@
     apart[0] = jnp.where(seen_apart, -1e30, 0.0)
     apart[1] = jnp.zeros((AREA, 3 * MAIN), F32)
 
-    def att_to(which):
-        return to_targets(spread_q_m, lambda m, w: nt(m, att_t[w]), which)
+    def att_wo(which):
+        return to_targets(spread_q_m, lambda m, w: nn(m, att_w[w]), which)
 
     gather_window(source, 3, own_n, margin_n)
     fetches[0].wait()
@@ -490,7 +487,7 @@
             def _():
                 for which in targets:
                     first, count_rows, _ = TARGETS[which]
-                    att_send[pl.ds(first - REACH, count_rows), :] = att_to(which).astype(BF)
+                    att_send[pl.ds(first - REACH, count_rows), :] = att_wo(which).astype(BF)
                 start(some)
 
         forward(w)
@@ -499,7 +496,7 @@
     lax.fori_loop(0, 4, forward_step, 0)
     for which in (0, 1):
         first, count_rows, _ = TARGETS[which]
-        attended[pl.ds(first, count_rows), :] = att_to(which)
+        attended[pl.ds(first, count_rows), :] = att_wo(which)
 
     links.arrived(idx_recv, 0, n)
     on_lane = iota((n, cap, 128), 2) == iota((n, cap, 128), 1)
@@ -616,18 +613,19 @@
         ds = scores_gradient(p, dp)
         late_dk = nn(ds, late_q)
         late_dv = nn(p.astype(BF), late_up)
-        out = nn(keys_t[w], ds)
-        dq_t[w, :, MAIN : 2 * MAIN] = (out * (heads.head_late * 0.125)).astype(BF)
+        late_dq = heads.late_out(ds, qkv[w, :, chans : 2 * chans])
+        dq_w[w, MAIN : 2 * MAIN, :] = late_dq * jnp.bfloat16(0.125)
         for pair in range(HEADS // 2):
             at = 128 * pair
             dp, after = after, dp_of(pair + 1)
-            ds, rounded = [], []
+            ds, rounded, out = [], [], []
             for h in range(2):
                 p = probs[w, :, at * 2 + MAIN * h : at * 2 + MAIN * (h + 1)]
                 ds.append(scores_gradient(p, dp[:, MAIN * h : MAIN * (h + 1)]))
                 rounded.append(p.astype(BF))
-                rows = slice(at + 64 * h, at + 64 * h + 64)
-                dq_t[w, rows, 0:MAIN] = (nn(keys_t[w, rows, :], ds[h]) * 0.125).astype(BF)
+                out.append(nn(keys_t[w, at + 64 * h : at + 64 * h + 64, :], ds[h]))
+            out = (jnp.concatenate(out, axis=0) * 0.125).astype(BF)
+            dq_w[w, 0:MAIN, at : at + 128] = out.T
             dk = nn(
                 jnp.concatenate(ds, axis=1), heads.stacked(pair_of(qkv, w, 0, MAIN, pair))
             )
@@ -640,7 +638,7 @@
             first, count_rows, _ = TARGETS[which]
             here = pl.ds(first, count_rows)
             proj_grad[here, 0:chans] = to_targets(
-                spread_q_m, lambda m, w: nt(m, dq_t[w]), which
+                spread_q_m, lambda m, w: nn(m, dq_w[w]), which
             ).astype(BF)
             proj_grad[here, chans : 2 * chans] = to_targets(
                 spread_m, lambda m, w: nn(m, dk_w[w]), which
@@ -716,12 +714,31 @@
     wait([own_store, misfit_store, back_store])
 
 
-def finish(own_part, back_part, costs, gradient, misfit):
-    gradient[...] = own_part[...]
-    returned = back_part[...].astype(F32)
-    for first, count_rows, at in RETURNED:
-        gradient[pl.ds(first, count_rows), :] += returned[at : at + count_rows]
-    misfit[...] = costs[...]
+def finish(own_hbm, back_hbm, costs_hbm, gradient, misfit, whole, back, costs, sems):
+    rows = CELLS // 6
+    parts = [pl.ds(first, rows) for first in range(0, CELLS, rows)]
+    ins = [pltpu.make_async_copy(own_hbm.at[p], whole.at[p], sems.at[i]) for i, p in enumerate(parts)]
+    outs = [
+        pltpu.make_async_copy(whole.at[p], gradient.at[p], sems.at[6 + i]) for i, p in enumerate(parts)
+    ]
+    more = [
+        pltpu.make_async_copy(back_hbm, back, sems.at[12]),
+        pltpu.make_async_copy(costs_hbm, costs, sems.at[13]),
+    ]
+    out = pltpu.make_async_copy(costs, misfit, sems.at[14])
+    start(more)
+    start(ins)
+    wait(more)
+    out.start()
+    returned = back[...].astype(F32)
+    for i in range(6):
+        ins[i].wait()
+        for first, count_rows, at in RETURNED:
+            if first // rows == i:
+                whole[pl.ds(first, count_rows), :] += returned[at : at + count_rows]
+        outs[i].start()
+    wait(outs)
+    out.wait()
 
 
 def shards(
@@ -745,7 +762,7 @@
     cap = 2 * feet // n
     slots = n * cap
     pack, gather, spread, spread_q = (jnp.asarray(m, BF) for m in selectors())
-    vmem, whole = pl.BlockSpec(memory_space=pltpu.VMEM), pl.BlockSpec(memory_space=pl.ANY)
+    whole = pl.BlockSpec(memory_space=pl.ANY)
     state = initial_state.reshape(CELLS, chans)
     gain = norm_gain.reshape(1, chans)
     tile_id = foot_tile.reshape(1, feet)
@@ -793,7 +810,7 @@
             room(4, AREA, 3 * chans),
             room(2, AREA, 3 * MAIN, dtype=F32),
             room(4, AREA, MAIN * (HEADS + 1), dtype=F32),
-            room(4, chans, 2 * MAIN),
+            room(4, 2 * MAIN, chans),
             room(MARGIN, chans),
             room(MARGIN, chans),
             room(CELLS, chans, dtype=F32),
@@ -820,7 +837,7 @@
             room(MARGIN, chans),
             room(4, AREA, chans),
             room(4, AREA, chans),
-            room(4, chans, 2 * MAIN),
+            room(4, 2 * MAIN, chans),
             room(4, chans, AREA),
             room(REACH + MARGIN, 3 * chans),
             room(MARGIN, chans),
@@ -854,8 +871,14 @@
     gradient, misfit = pl.pallas_call(
         finish,
         out_shape=(shape(CELLS, chans, dtype=F32), shape(1, feet, dtype=F32)),
-        in_specs=[vmem] * 3,
-        out_specs=(vmem, vmem),
+        in_specs=[whole] * 3,
+        out_specs=(whole, whole),
+        scratch_shapes=[
+            room(CELLS, chans, dtype=F32),
+            room(MARGIN, chans),
+            room(1, feet, dtype=F32),
+            pltpu.SemaphoreType.DMA((15,)),
+        ],
     )(own_part, back_part, costs)
     return gradient.reshape(initial_state.shape), misfit.reshape(feet)
 

time: 60.8 us -> 60.2 us (level)
  Pallas kernels: 59.3 us -> 58.6 us
where the time goes in v4:
time: 60.2 us; the launch traced here: 60.1 us
  Pallas kernels  58.6 us (97%)
  between operations  1.45 us (2%)
    pallas_call x1, Pallas kernels, shards(): pl.pallas_call(functools.partial(kernel, lats, lons, cap), out_shape=(sha...  56.4 us
    pallas_call x1, Pallas kernels, shards(): pl.pallas_call(finish, out_shape=(shape(CELLS, chans, dtype=F32), shape(1...  2.22 us

profile of v4, /device:TPU:25, one launch (start us, length us, event | category | flops | bytes accessed | tf_op | source)
XLA Modules:
  0.0 60.1 jit_solution(8160994517589236462)
XLA Ops:
  1.3 56.4 %shard_map.158 = (f32[576,512]{1,0:T(8,128)}, bf16[272,512]{1,0:T(8,128)(2,1)}, f32[1,512]{1,0:T(1,128)}) custom-call(bf16[576,512]{1,0:T(8,128)(2,1)} %bitcast.9, f32[1,512]{1,0:T(1,128)} %bitcast.10, bf16[512,1536]{1,0:T(8,128)(2,1)} %w_in_hbm.1, bf16[512,512]{1,0:T(8,128)(2,1)} %w_out_hbm.1, bf16[512,1024]{1,0:T(8,128)(2,1)} %obs_in_hbm.1, ...), custom_call_target="tpu_custom_call" | custom-call | tf_op jit(solution)/shard_map/pallas_call | solution.py:778
  57.7 2.2 %shard_map.159 = (f32[576,512]{1,0:T(8,128)}, f32[1,512]{1,0:T(1,128)}) custom-call(f32[576,512]{1,0:T(8,128)} %get-tuple-element.7.own_hbm, bf16[272,512]{1,0:T(8,128)(2,1)} %get-tuple-element.8.back_hbm, f32[1,512]{1,0:T(1,128)} %get-tuple-element.9.costs_hbm), custom_call_target="tpu_custom_call" | custom-call | tf_op jit(solution)/shard_map/pallas_call | solution.py:871

commit v5 on v4

--- a/solution.py
+++ b/solution.py
@@ -136,13 +136,25 @@
         return lax.rem(self.lat + up + lats, lats), lax.rem(self.lon + right + lons, lons)
 
     def away_by(self, d):
-        return self.around(lax.rem(d, self.lats), d // self.lats)
+        return self.around(d // self.lons, d % self.lons)
 
     def greet(self, device):
         pl.semaphore_signal(self.barrier, inc=1, device_id=device, device_id_type=MESH)
 
+    def others(self, act):
+        steps = (self.n - 1) // 7
+
+        def seven(k, carry):
+            for j in range(7):
+                act(1 + 7 * k + j)
+            return carry
+
+        lax.fori_loop(0, steps, seven, 0)
+        for d in range(1 + 7 * steps, self.n):
+            act(d)
+
     def greet_all(self):
-        each(1, self.n, lambda d: self.greet(self.away_by(d)))
+        self.others(lambda d: self.greet(self.away_by(d)))
 
     def met_all(self):
         pl.semaphore_wait(self.barrier, self.n - 1)
@@ -174,32 +186,22 @@
         self.copy(self.foot_sem, i, rest, rest, self.around(1, 0)).wait()
 
     def to_all(self, send, into, i):
-        each(
-            1,
-            self.n,
-            lambda d: self.copy(self.foot_sem, i, send.at[d], into.at[d], self.away_by(d)).start(),
+        self.others(
+            lambda d: self.copy(self.foot_sem, i, send.at[d], into.at[d], self.away_by(d)).start()
         )
         into[0] = send[0]
 
-    def back_lat(self, send, into, i):
-        each(
-            1,
-            self.lats,
-            lambda step: self.copy(
-                self.foot_sem, i, send.at[:, step], into.at[step], self.around(-step, 0)
-            ).start(),
-        )
+    def along_lon(self, send, into, i, way):
+        for step in range(1, self.lons):
+            device = self.around(0, way * step)
+            self.copy(self.foot_sem, i, send.at[:, step], into.at[step], device).start()
         into[0] = send[:, 0]
 
-    def back_lon(self, mid, into, i):
-        each(
-            1,
-            self.lons,
-            lambda step: self.copy(
-                self.foot_sem, i, mid.at[:, step], into.at[step], self.around(0, -step)
-            ).start(),
-        )
-        into[0] = mid[:, 0]
+    def along_lat(self, send, into, i, way):
+        for step in range(1, self.lats):
+            device = self.around(way * step, 0)
+            self.copy(self.foot_sem, i, send.at[:, step], into.at[step], device).start()
+        into[0] = send[:, 0]
 
 
 def footprint_places(links, tile_id, count, cap):
@@ -208,7 +210,7 @@
     tile_lat = jnp.floor((tile_id[...].astype(F32) + 0.5) * (1.0 / lons)).astype(jnp.int32)
     up, right = tile_lat - links.lat, tile_id[...] - tile_lat * lons - links.lon
     up, right = jnp.where(up < 0, up + lats, up), jnp.where(right < 0, right + lons, right)
-    away = right * lats + up
+    away = up * lons + right
     live = iota((1, feet), 1) < count[...]
     named = (iota((n, feet), 0) == away).astype(F32)
     before = (iota((feet, feet), 0) < iota((feet, feet), 1)).astype(F32).astype(BF)
@@ -319,6 +321,7 @@
     obs_send,
     obs_recv,
     idx_send,
+    idx_mid,
     idx_recv,
     mis_send,
     mis_mid,
@@ -400,14 +403,14 @@
         cell = jnp.sum(block * cell_value, axis=1, keepdims=True) - 1.0
         cell = jnp.where(on_lane, cell.reshape(4, cap, 1), 0.0)
         cells.append(jnp.sum(cell, axis=1, keepdims=True))
-    idx_send[...] = jnp.concatenate(cells, axis=0)
+    idx_send[...] = jnp.concatenate(cells, axis=0).reshape(lats, lons, 1, 128)
+    links.along_lon(idx_send, idx_mid, 0, 1)
     fetches[9].wait()
     rows = nn(chosen[...], observed[...])
     half = rows.shape[1] // 2
     rows = rows.reshape(n, cap, 2 * half)
     obs_send[...] = jnp.concatenate([rows[:, :, :half], rows[:, :, half:]], axis=1).astype(BF)
 
-    links.to_all(idx_send, idx_recv, 0)
     links.to_all(obs_send, obs_recv, 1)
 
     normalize(state, gain[...], own_n)
@@ -478,6 +481,8 @@
     place(range(3))
     project(0, 3)
     fetches[2].wait()
+    links.arrived(idx_mid, 0, lons)
+    links.along_lat(idx_mid, idx_recv, 3, 1)
     att_copies = links.pieces(3, att_send, att_recv, -1)
 
     def forward_step(w, carry):
@@ -498,9 +503,9 @@
         first, count_rows, _ = TARGETS[which]
         attended[pl.ds(first, count_rows), :] = att_wo(which)
 
-    links.arrived(idx_recv, 0, n)
+    links.arrived(idx_recv, 3, lats)
     on_lane = iota((n, cap, 128), 2) == iota((n, cap, 128), 1)
-    spots = jnp.where(on_lane, idx_recv[...], 0.0)
+    spots = jnp.where(on_lane, idx_recv[...].reshape(n, 1, 128), 0.0)
     spots = jnp.sum(spots, axis=2, keepdims=True).reshape(slots, 1)
     pick = (iota((8, 128), 1) == 0).astype(F32)
     spots_row = lax.dot_general(
@@ -564,8 +569,8 @@
             cost = 0.5 * jnp.sum(residual * residual, axis=1, keepdims=True)
             cost = jnp.where(lanes, cost.reshape(step // cap, cap, 1), 0.0)
             costs.append(jnp.sum(cost, axis=1, keepdims=True))
-        blocks = pl.ds(c * (lons // 2), lons // 2)
-        mis_send[blocks] = jnp.concatenate(costs, axis=0).reshape(lons // 2, lats, 1, 128)
+        blocks = pl.ds(c * (lats // 2), lats // 2)
+        mis_send[blocks] = jnp.concatenate(costs, axis=0).reshape(lats // 2, lons, 1, 128)
         for cols in quarters:
             whole = nt(residuals[here, :], obs_out[cols, :])
             for first in range(0, chunk, step):
@@ -583,7 +588,7 @@
     packed_g[...] = nt(to_send, w_out[...]).astype(BF)
     grad_copies = links.pieces(6, packed_g, margin_g, 1)
     start(grad_copies)
-    links.back_lat(mis_send, mis_mid, 2)
+    links.along_lon(mis_send, mis_mid, 2, -1)
     state_grad[...] = nn(back[...], foot_grad[...])
     att_grad[...] = nt(state_grad[pl.ds(0, REACH), :].astype(BF), w_out[...]).astype(BF)
 
@@ -673,8 +678,8 @@
 
         @pl.when(step == 2)
         def _():
-            links.arrived(mis_mid, 2, lats)
-            links.back_lon(mis_mid, mis_recv, 3)
+            links.arrived(mis_mid, 2, lons)
+            links.along_lat(mis_mid, mis_recv, 4, -1)
 
         @pl.when(step == 3)
         def _():
@@ -696,7 +701,7 @@
     own_store = pltpu.make_async_copy(own_part, own_part_hbm, store_sem.at[0])
     own_store.start()
 
-    links.arrived(mis_recv, 3, lons)
+    links.arrived(mis_recv, 4, lats)
     costs = lax.dot_general(
         mis_recv[...].reshape(n, 128),
         named,
@@ -817,11 +822,12 @@
             room(CELLS, chans),
             room(n, 2 * cap, seen // 2),
             room(n, 2 * cap, seen // 2),
-            room(n, 1, 128, dtype=F32),
-            room(n, 1, 128, dtype=F32),
+            room(lats, lons, 1, 128, dtype=F32),
             room(lons, lats, 1, 128, dtype=F32),
             room(lats, lons, 1, 128, dtype=F32),
+            room(lats, lons, 1, 128, dtype=F32),
             room(lons, lats, 1, 128, dtype=F32),
+            room(lats, lons, 1, 128, dtype=F32),
             room(slots, feet),
             room(slots, obs_in_weight.shape[1], dtype=F32),
             room(slots, obs_in_weight.shape[1]),
@@ -844,7 +850,7 @@
             room(MARGIN, chans),
             room(CELLS, chans, dtype=F32),
             pltpu.SemaphoreType.DMA((24,)),
-            pltpu.SemaphoreType.DMA((8,)),
+            pltpu.SemaphoreType.DMA((10,)),
             pltpu.SemaphoreType.DMA((15,)),
             pltpu.SemaphoreType.DMA((3,)),
         ],

time: 60.2 us -> 62.1 us (1.032)
  Pallas kernels: 58.6 us -> 60.5 us
    pallas_call x1, Pallas kernels: 56.4 us -> 58.3 us  [shards(): pl.pallas_call(functools.partial(kernel, lats, lons, cap), out_shape=(sha...]
where the time goes in v5:
time: 62.1 us; the launch traced here: 62 us
  Pallas kernels  60.5 us (97%)
  between operations  1.45 us (2%)
    pallas_call x1, Pallas kernels, shards(): pl.pallas_call(functools.partial(kernel, lats, lons, cap), out_shape=(sha...  58.3 us
    pallas_call x1, Pallas kernels, shards(): pl.pallas_call(finish, out_shape=(shape(CELLS, chans, dtype=F32), shape(1...  2.22 us

profile of v5, /device:TPU:25, one launch (start us, length us, event | category | flops | bytes accessed | tf_op | source)
XLA Modules:
  0.0 62.0 jit_solution(15738038074716981576)
XLA Ops:
  1.3 58.3 %shard_map.158 = (f32[576,512]{1,0:T(8,128)}, bf16[272,512]{1,0:T(8,128)(2,1)}, f32[1,512]{1,0:T(1,128)}) custom-call(bf16[576,512]{1,0:T(8,128)(2,1)} %bitcast.9, f32[1,512]{1,0:T(1,128)} %bitcast.10, bf16[512,1536]{1,0:T(8,128)(2,1)} %w_in_hbm.1, bf16[512,512]{1,0:T(8,128)(2,1)} %w_out_hbm.1, bf16[512,1024]{1,0:T(8,128)(2,1)} %obs_in_hbm.1, ...), custom_call_target="tpu_custom_call" | custom-call | tf_op jit(solution)/shard_map/pallas_call | solution.py:783
  59.6 2.2 %shard_map.159 = (f32[576,512]{1,0:T(8,128)}, f32[1,512]{1,0:T(1,128)}) custom-call(f32[576,512]{1,0:T(8,128)} %get-tuple-element.7.own_hbm, bf16[272,512]{1,0:T(8,128)(2,1)} %get-tuple-element.8.back_hbm, f32[1,512]{1,0:T(1,128)} %get-tuple-element.9.costs_hbm), custom_call_target="tpu_custom_call" | custom-call | tf_op jit(solution)/shard_map/pallas_call | solution.py:877

commit v6 on v4

--- a/solution.py
+++ b/solution.py
@@ -1,4 +1,5 @@
 import functools
+import math
 
 import jax
 import jax.numpy as jnp
@@ -174,11 +175,13 @@
         self.copy(self.foot_sem, i, rest, rest, self.around(1, 0)).wait()
 
     def to_all(self, send, into, i):
-        each(
-            1,
-            self.n,
-            lambda d: self.copy(self.foot_sem, i, send.at[d], into.at[d], self.away_by(d)).start(),
-        )
+        stride = 45 if math.gcd(45, self.n) == 1 else 1
+
+        def one(k):
+            d = lax.rem(k * stride, self.n)
+            self.copy(self.foot_sem, i, send.at[d], into.at[d], self.away_by(d)).start()
+
+        each(1, self.n, one)
         into[0] = send[0]
 
     def back_lat(self, send, into, i):

time: 60.2 us -> 60.9 us (1.012)
  Pallas kernels: 58.6 us -> 59.4 us
    pallas_call x1, Pallas kernels: 56.4 us -> 57.1 us  [shards(): pl.pallas_call(functools.partial(kernel, lats, lons, cap), out_shape=(sha...]
where the time goes in v6:
time: 60.9 us; the launch traced here: 60.8 us
  Pallas kernels  59.4 us (98%)
  between operations  1.45 us (2%)
    pallas_call x1, Pallas kernels, shards(): pl.pallas_call(functools.partial(kernel, lats, lons, cap), out_shape=(sha...  57.1 us
    pallas_call x1, Pallas kernels, shards(): pl.pallas_call(finish, out_shape=(shape(CELLS, chans, dtype=F32), shape(1...  2.22 us

profile of v6, /device:TPU:25, one launch (start us, length us, event | category | flops | bytes accessed | tf_op | source)
XLA Modules:
  0.0 60.8 jit_solution(17993581293218800363)
XLA Ops:
  1.3 57.1 %shard_map.158 = (f32[576,512]{1,0:T(8,128)}, bf16[272,512]{1,0:T(8,128)(2,1)}, f32[1,512]{1,0:T(1,128)}) custom-call(bf16[576,512]{1,0:T(8,128)(2,1)} %bitcast.9, f32[1,512]{1,0:T(1,128)} %bitcast.10, bf16[512,1536]{1,0:T(8,128)(2,1)} %w_in_hbm.1, bf16[512,512]{1,0:T(8,128)(2,1)} %w_out_hbm.1, bf16[512,1024]{1,0:T(8,128)(2,1)} %obs_in_hbm.1, ...), custom_call_target="tpu_custom_call" | custom-call | tf_op jit(solution)/shard_map/pallas_call | solution.py:781
  58.4 2.2 %shard_map.159 = (f32[576,512]{1,0:T(8,128)}, f32[1,512]{1,0:T(1,128)}) custom-call(f32[576,512]{1,0:T(8,128)} %get-tuple-element.7.own_hbm, bf16[272,512]{1,0:T(8,128)(2,1)} %get-tuple-element.8.back_hbm, f32[1,512]{1,0:T(1,128)} %get-tuple-element.9.costs_hbm), custom_call_target="tpu_custom_call" | custom-call | tf_op jit(solution)/shard_map/pallas_call | solution.py:874
